TPU v7x, 32 devices: a whole 2x2x4 slice. The times are simulated.
32 devices in a mesh: section: 2 (over core), dp: 16 (over z, y, x).
Axes of the slice: x: 2, y: 2, z: 4, core: 2. Of those that a mesh axis runs over, the one named last changes fastest.
Arguments:
- inputs: bfloat16 [32768, 768], P('dp'), may hold values from -6 to 6
- out_grad: bfloat16 [32768, 768], P('dp'), may hold values from -6 to 6
- picks: int32 [32, 128], P('dp'), may hold values from 0 to 1023, as said below
- valid: int32 [32, 128], P('dp'), may hold values from 0 to 1, as said below
- router: float32 [768], replicated, may hold values from -0.21875 to 0.21875
- gain_attn: float32 [2, 768], P('section'), may hold values from 0.1 to 1.9
- w_qkv: bfloat16 [2, 768, 2304], P('section'), may hold values from -0.21875 to 0.21875
- w_out: bfloat16 [2, 768, 768], P('section'), may hold values from -0.875 to 0.875
- gain_mlp: float32 [2, 768], P('section'), may hold values from 0.1 to 1.9
- w_in: bfloat16 [2, 768, 3072], P('section'), may hold values from -0.21875 to 0.21875
- w_back: bfloat16 [2, 3072, 768], P('section'), may hold values from -0.109375 to 0.109375
Outputs:
- block_ends: bfloat16 [2, 32768, 768], P('section', 'dp')
- router_grad: float32 [768], replicated
- gain_attn_grad: float32 [2, 768], P('section', 'dp')
- w_qkv_grad: float32 [2, 768, 2304], P('section', 'dp')
- w_out_grad: float32 [2, 768, 768], P('section', 'dp')
- gain_mlp_grad: float32 [2, 768], P('section', 'dp')
- w_in_grad: float32 [2, 768, 3072], P('section', 'dp')
- w_back_grad: float32 [2, 3072, 768], P('section', 'dp')
Inputs may be any that keep to these rules, and one draw needn't show every extreme that they name: `picks`: each row holds 128 different positions of its sequence, in increasing order. `valid`: each row has between 32 and 128 slots equal to 1; some row has all 128.
All inputs are finite; a program needn't handle non-finite values.
Results may differ from a plain program's by a relative error of at most 0.02.
Values may be sent and summed in bfloat16 or wider, within the bound.
No kernel may reach another device: no remote copies, remote signals or barrier semaphores. Data moves between devices by JAX's collectives and lax.ppermute only.
A program may use at most 384 MiB of HBM per device.

v0:
```python
import jax
import jax.numpy as jnp
from jax import lax
from jax.sharding import PartitionSpec as P

HEADS = 12
HEAD_DIM = 64


eps = 1e-06
highest = lax.Precision.HIGHEST


def shifted(value, axis, steps):
    count = lax.axis_size(axis)
    initial, last = (max(0, -steps), min(count, count - steps))
    return lax.ppermute(value, axis, [(source, source + steps) for source in range(initial, last)])


def norm_rows(row_data, gain):
    return row_data * lax.rsqrt(jnp.mean(row_data * row_data, axis=-1, keepdims=True) + eps) * gain


def head_split(packed, which):
    row_count = packed.shape[0]
    return packed[:, which * HEADS * HEAD_DIM : (which + 1) * HEADS * HEAD_DIM].reshape(
        row_count, HEADS, HEAD_DIM
    )


def attend_forward(packed, allowed):
    row_count = packed.shape[0]
    queries = head_split(packed, 0)
    key_heads = head_split(packed, 1)
    value_heads = head_split(packed, 2)
    block_rows = min(512, row_count)
    factor = HEAD_DIM ** (-0.5)

    def attend_block(block_index):
        first_row = block_index * block_rows
        query_block = lax.dynamic_slice_in_dim(queries, first_row, block_rows, 0)
        scores = (
            jnp.einsum("qhd,khd->hqk", query_block, key_heads, preferred_element_type=jnp.float32)
            * factor
        )
        scores = jnp.where(allowed(first_row, block_rows)[None], scores, -1e30)
        row_max = jnp.max(scores, axis=-1, keepdims=True)
        exponent = jnp.exp(scores - row_max)
        row_total = jnp.sum(exponent, axis=-1, keepdims=True)
        attn_probs = (exponent / row_total).astype(jnp.bfloat16)
        mixed_heads = jnp.einsum(
            "hqk,khd->qhd", attn_probs, value_heads, preferred_element_type=jnp.float32
        )
        mixed_heads = mixed_heads.astype(jnp.bfloat16).reshape(block_rows, HEADS * HEAD_DIM)
        return (mixed_heads, (row_max + jnp.log(row_total))[..., 0])

    mixed_heads, logsum = lax.map(attend_block, jnp.arange(row_count // block_rows))
    return (mixed_heads.reshape(row_count, HEADS * HEAD_DIM), logsum)


def attend_backward(packed, logsum, grad_mixed, allowed):
    row_count = packed.shape[0]
    queries = head_split(packed, 0)
    key_heads = head_split(packed, 1)
    value_heads = head_split(packed, 2)
    grad_heads = grad_mixed.reshape(row_count, HEADS, HEAD_DIM)
    block_rows = min(512, row_count)
    factor = HEAD_DIM ** (-0.5)

    def attend_block(running, block_index):
        grad_key, grad_value = running
        first_row = block_index * block_rows
        query_block = lax.dynamic_slice_in_dim(queries, first_row, block_rows, 0)
        grad_block = lax.dynamic_slice_in_dim(grad_heads, first_row, block_rows, 0)
        scores = (
            jnp.einsum("qhd,khd->hqk", query_block, key_heads, preferred_element_type=jnp.float32)
            * factor
        )
        allowed_now = allowed(first_row, block_rows)[None]
        attn_probs = jnp.where(allowed_now, jnp.exp(scores - logsum[block_index][..., None]), 0.0)
        low_probs = attn_probs.astype(jnp.bfloat16)
        grad_probs = jnp.einsum(
            "qhd,khd->hqk", grad_block, value_heads, preferred_element_type=jnp.float32
        )
        grad_scores = attn_probs * (
            grad_probs - jnp.sum(grad_probs * attn_probs, axis=-1, keepdims=True)
        )
        low_scores = grad_scores.astype(jnp.bfloat16)
        grad_query = (
            jnp.einsum("hqk,khd->qhd", low_scores, key_heads, preferred_element_type=jnp.float32)
            * factor
        )
        grad_key = (
            grad_key
            + jnp.einsum(
                "hqk,qhd->khd", low_scores, query_block, preferred_element_type=jnp.float32
            )
            * factor
        )
        grad_value = grad_value + jnp.einsum(
            "hqk,qhd->khd", low_probs, grad_block, preferred_element_type=jnp.float32
        )
        return ((grad_key, grad_value), grad_query)

    zero_heads = jnp.zeros((row_count, HEADS, HEAD_DIM), jnp.float32)
    sums_now, grad_query = lax.scan(
        attend_block, (zero_heads, zero_heads), jnp.arange(row_count // block_rows)
    )
    grad_query = grad_query.reshape(row_count, HEADS * HEAD_DIM)
    grad_key = sums_now[0].reshape(row_count, HEADS * HEAD_DIM)
    grad_value = sums_now[1].reshape(row_count, HEADS * HEAD_DIM)
    return jnp.concatenate([grad_query, grad_key, grad_value], axis=1).astype(jnp.bfloat16)


def block_forward(row_data, weights, allowed):
    gain_attn, w_qkv, w_out, gain_mlp, w_in, w_back = weights
    normed = norm_rows(row_data, gain_attn).astype(jnp.bfloat16)
    packed = jnp.dot(normed, w_qkv, preferred_element_type=jnp.float32).astype(jnp.bfloat16)
    mixed_heads, logsum = attend_forward(packed, allowed)
    attn_out = jnp.dot(mixed_heads, w_out, preferred_element_type=jnp.float32)
    middle_rows = row_data + attn_out
    normed_mid = norm_rows(middle_rows, gain_mlp).astype(jnp.bfloat16)
    hidden_pre = jnp.dot(normed_mid, w_in, preferred_element_type=jnp.float32)
    hidden_act = jax.nn.gelu(hidden_pre).astype(jnp.bfloat16)
    ffn_out = jnp.dot(hidden_act, w_back, preferred_element_type=jnp.float32)
    kept = (normed, packed, mixed_heads, logsum, middle_rows, normed_mid, hidden_pre, hidden_act)
    return (attn_out + ffn_out, kept)


def block_backward(row_data, weights, kept, grad_branch, allowed):
    gain_attn, w_qkv, w_out, gain_mlp, w_in, w_back = weights
    normed, packed, mixed_heads, logsum, middle_rows, normed_mid, hidden_pre, hidden_act = kept
    grad_ffn = grad_branch.astype(jnp.bfloat16)
    grad_w_back = jnp.einsum("nf,nd->fd", hidden_act, grad_ffn, preferred_element_type=jnp.float32)
    grad_act = jnp.einsum("nd,fd->nf", grad_ffn, w_back, preferred_element_type=jnp.float32)
    gelu_out, gelu_pull = jax.vjp(jax.nn.gelu, hidden_pre)
    grad_hidden = gelu_pull(grad_act)[0].astype(jnp.bfloat16)
    grad_w_in = jnp.einsum("nd,nf->df", normed_mid, grad_hidden, preferred_element_type=jnp.float32)
    grad_normed_mid = jnp.einsum("nf,df->nd", grad_hidden, w_in, preferred_element_type=jnp.float32)
    norm_out, norm_pull = jax.vjp(norm_rows, middle_rows, gain_mlp)
    grad_middle, grad_gain_mlp = norm_pull(grad_normed_mid)
    grad_attn = (grad_branch + grad_middle).astype(jnp.bfloat16)
    grad_w_out = jnp.einsum("nd,ne->de", mixed_heads, grad_attn, preferred_element_type=jnp.float32)
    grad_mixed = jnp.einsum(
        "ne,de->nd", grad_attn, w_out, preferred_element_type=jnp.float32
    ).astype(jnp.bfloat16)
    grad_packed = attend_backward(packed, logsum, grad_mixed, allowed)
    grad_w_qkv = jnp.einsum("nd,ne->de", normed, grad_packed, preferred_element_type=jnp.float32)
    grad_normed = jnp.einsum("ne,de->nd", grad_packed, w_qkv, preferred_element_type=jnp.float32)
    first_out, first_pull = jax.vjp(norm_rows, row_data, gain_attn)
    grad_rows, grad_gain_attn = first_pull(grad_normed)
    grad_tuple = (grad_gain_attn, grad_w_qkv, grad_w_out, grad_gain_mlp, grad_w_in, grad_w_back)
    return (grad_middle + grad_rows, grad_tuple)


def shards(inputs, out_grad, picks, valid, router, gain_attn, w_qkv, w_out, gain_mlp, w_in, w_back):
    weights = (gain_attn[0], w_qkv[0], w_out[0], gain_mlp[0], w_in[0], w_back[0])
    micro_count = picks.shape[0]
    capacity = picks.shape[1]
    seq_len = inputs.shape[0] // micro_count
    model_width = inputs.shape[1]
    section_index = lax.axis_index("section")
    zero_grads = tuple((jnp.zeros(weight.shape, jnp.float32) for weight in weights))
    zero_router = jnp.zeros((model_width,), jnp.float32)
    zero_fwd = jnp.zeros((capacity, model_width), jnp.bfloat16)
    zero_bwd = jnp.zeros((seq_len, model_width), jnp.bfloat16)
    slot_ids = jnp.arange(capacity)
    places = jnp.arange(seq_len)

    def causal(first_row, block_rows):
        rows_here = first_row + jnp.arange(block_rows)
        return places[None, :] <= rows_here[:, None]

    def routed_setup(micro_index):
        seq_picks = picks[micro_index]
        seq_valid = valid[micro_index]
        seq_rows = lax.dynamic_slice_in_dim(inputs, micro_index * seq_len, seq_len, 0)
        chosen = jnp.take(seq_rows, seq_picks, axis=0).astype(jnp.float32)

        def selected(first_row, block_rows):
            query_slots = first_row + jnp.arange(block_rows)
            usable = (seq_valid[None, :] > 0) | (slot_ids[None, :] == query_slots[:, None])
            return (seq_picks[None, :] <= seq_picks[:, None]) & usable

        gates = jax.nn.sigmoid(jnp.dot(chosen, router, precision=highest))
        slot_mask = seq_valid.astype(jnp.float32)
        branch, kept = block_forward(chosen, weights, selected)
        return (seq_picks, chosen, selected, gates, slot_mask, branch, kept)

    def routed_tick(tick_index, inbox_fwd, inbox_bwd, ends_buffer):

        def forward_part(micro_index):
            setup = routed_setup(micro_index)
            return ((setup[3] * setup[4])[:, None] * setup[5]).astype(jnp.bfloat16)

        def skip_forward(micro_index):
            return zero_fwd

        send_fwd = lax.cond(
            tick_index < micro_count,
            forward_part,
            skip_forward,
            jnp.minimum(tick_index, micro_count - 1),
        )

        def backward_part(ends_now):
            micro_index = jnp.maximum(tick_index - 2, 0)
            seq_picks, chosen, selected, gates, slot_mask, branch, kept = routed_setup(micro_index)
            grad_middle = inbox_bwd.astype(jnp.float32)
            grad_sel = jnp.take(grad_middle, seq_picks, axis=0)
            grad_logit = jnp.sum(grad_sel * branch, axis=-1) * slot_mask * gates * (1.0 - gates)
            grad_rows, grad_tuple = block_backward(
                chosen, weights, kept, grad_sel * (gates * slot_mask)[:, None], selected
            )
            grad_rows = grad_rows + grad_logit[:, None] * router[None, :]
            grad_router = jnp.dot(grad_logit, chosen, precision=highest)
            grad_inputs = grad_middle.at[seq_picks].add(grad_rows).astype(jnp.bfloat16)
            ends_now = lax.dynamic_update_slice_in_dim(
                ends_now, grad_inputs, micro_index * seq_len, 0
            )
            return (ends_now, grad_tuple, grad_router)

        def skip_backward(ends_now):
            return (ends_now, zero_grads, zero_router)

        ends_buffer, grad_tuple, grad_router = lax.cond(
            tick_index >= 2, backward_part, skip_backward, ends_buffer
        )
        return (send_fwd, zero_bwd, ends_buffer, grad_tuple, grad_router)

    def dense_tick(tick_index, inbox_fwd, inbox_bwd, ends_buffer):

        def dense_part(ends_now):
            micro_index = jnp.clip(tick_index - 1, 0, micro_count - 1)
            seq_rows = lax.dynamic_slice_in_dim(inputs, micro_index * seq_len, seq_len, 0).astype(
                jnp.float32
            )
            middle = seq_rows.at[picks[micro_index]].add(inbox_fwd.astype(jnp.float32))
            branch, kept = block_forward(middle, weights, causal)
            ends_now = lax.dynamic_update_slice_in_dim(
                ends_now, (middle + branch).astype(jnp.bfloat16), micro_index * seq_len, 0
            )
            grad_result = lax.dynamic_slice_in_dim(
                out_grad, micro_index * seq_len, seq_len, 0
            ).astype(jnp.float32)
            grad_rows, grad_tuple = block_backward(middle, weights, kept, grad_result, causal)
            return ((grad_result + grad_rows).astype(jnp.bfloat16), ends_now, grad_tuple)

        def skip_dense(ends_now):
            return (zero_bwd, ends_now, zero_grads)

        working = (tick_index >= 1) & (tick_index <= micro_count)
        send_bwd, ends_buffer, grad_tuple = lax.cond(working, dense_part, skip_dense, ends_buffer)
        return (zero_fwd, send_bwd, ends_buffer, grad_tuple, zero_router)

    def tick_work(tick_index, state_now):
        inbox_fwd, inbox_bwd, ends_buffer, totals, router_sum = state_now
        send_fwd, send_bwd, ends_buffer, grad_tuple, grad_router = lax.cond(
            section_index == 0,
            routed_tick,
            dense_tick,
            tick_index,
            inbox_fwd,
            inbox_bwd,
            ends_buffer,
        )
        inbox_fwd = shifted(send_fwd, "section", 1)
        inbox_bwd = shifted(send_bwd, "section", -1)
        return ((inbox_fwd, inbox_bwd, ends_buffer, totals, router_sum + grad_router), grad_tuple)

    def tick_step(tick_index, state_now):
        state_next, grad_tuple = tick_work(tick_index, state_now)
        totals = tuple((running + fresh for running, fresh in zip(state_next[3], grad_tuple)))
        return state_next[:3] + (totals,) + state_next[4:]

    start_state = (
        zero_fwd,
        zero_bwd,
        jnp.zeros(inputs.shape, jnp.bfloat16),
        zero_grads,
        zero_router,
    )
    final_state = lax.fori_loop(0, micro_count + 2, tick_step, start_state)
    totals = lax.psum_scatter(final_state[3], "dp", scatter_dimension=0, tiled=True)
    ends_buffer = final_state[2]
    router_sum = lax.psum(final_state[4], ("section", "dp"))
    return (
        ends_buffer[None],
        router_sum,
        totals[0][None],
        totals[1][None],
        totals[2][None],
        totals[3][None],
        totals[4][None],
        totals[5][None],
    )


def solution(mesh):
    placed = (
        P("dp", None),
        P("dp", None),
        P("dp", None),
        P("dp", None),
        P(),
        P("section", None),
        P("section", None, None),
        P("section", None, None),
        P("section", None),
        P("section", None, None),
        P("section", None, None),
    )
    return jax.shard_map(
        shards,
        mesh=mesh,
        in_specs=placed,
        out_specs=(
            P("section", "dp", None),
            P(),
            P("section", "dp"),
            P("section", "dp", None),
            P("section", "dp", None),
            P("section", "dp"),
            P("section", "dp", None),
            P("section", "dp", None),
        ),
        check_vma=False,
    )
```

profile of v0, /device:TPU:0, one launch (start us, length us, event | category | flops | bytes accessed | tf_op | source)
XLA Modules:
  0.0 1803.4 jit_solution(2648662456228509272)
XLA Ops:
  10.5 1145.0 %while.69 = (s32[]{:T(128)}, bf16[128,768]{1,0:T(8,128)(2,1)S(1)}, bf16[1024,768]{1,0:T(8,128)(2,1)}, bf16[2048,768]{1,0:T(8,128)(2,1)}, f32[768]{0:T(1024)}, /*...) while((s32[]{:T(128)}, bf16[128,768]{1,0:T(8,128)(2,1)S(1)}, ...), condition=%wide.region_38.40_spmd.clone.clone, body=%wide.region_0.39_spmd.clone.clone.sunk | while | flops 49509502976 | bytes 1038052032 | solution.py:283
  11.6 61.5 %conditional.7 = (bf16[128,768]{1,0:T(8,128)(2,1)}, bf16[1024,768]{1,0:T(8,128)(2,1)}, bf16[2048,768]{1,0:T(8,128)(2,1)}, f32[768]{0:T(1024)}, f32[768,2304]{1,0...) conditional(s32[]{:T(128)} %convert_element_type.304, ...), branch_computations={%region_1.17_spmd, %region_18.38_spmd} | conditional | flops 49495343104 | bytes 938855104 | solution.py:258
  24.4 27.6 %conditional.1 = (bf16[128,768]{1,0:T(8,128)(2,1)}) conditional(s32[]{:T(128)} %convert_element_type.171, () %tuple.67, (s32[]{:T(128)}, bf16[2048,768]{1,0:T(8,128)(2,1)}, s32[2,128]{1,0:T(2,128)}, f32[768]{0:T(1024)}, s32[2,128]{1,0:T(2,128)}, /*index=5*/f32[1,768]{1,0:T(1,128)}, bf16[768,2304]{1,0:T(8,128)(2,1)}, s32[128]{0:T(128)}, ...), branch_computations={%region_19.18_spmd, %region_20.0_spmd} | conditional | flops 1896747904 | bytes 45341504 | solution.py:199
  32.8 2.7 constant_dynamic-slice_fusion.3
  35.5 3.4 gather_fusion.2
  45.7 6.3 fusion.72
  52.0 17.0 conditional.2
  55.3 3.3 broadcast_in_dim.218
  58.7 4.1 broadcast_in_dim.221
  62.8 4.8 broadcast_in_dim.220
  75.7 3.4 select_add_fusion.15
  79.1 6.9 select_add_fusion.14
  85.9 10.3 select_add_fusion.17
  97.0 8.6 select_add_fusion.18
  108.8 61.5 %conditional.7 = (bf16[128,768]{1,0:T(8,128)(2,1)}, bf16[1024,768]{1,0:T(8,128)(2,1)}, bf16[2048,768]{1,0:T(8,128)(2,1)}, f32[768]{0:T(1024)}, f32[768,2304]{1,0...) conditional(s32[]{:T(128)} %convert_element_type.304, ...), branch_computations={%region_1.17_spmd, %region_18.38_spmd} | conditional | flops 49495343104 | bytes 938855104 | solution.py:258
  121.8 27.6 %conditional.1 = (bf16[128,768]{1,0:T(8,128)(2,1)}) conditional(s32[]{:T(128)} %convert_element_type.171, () %tuple.67, (s32[]{:T(128)}, bf16[2048,768]{1,0:T(8,128)(2,1)}, s32[2,128]{1,0:T(2,128)}, f32[768]{0:T(1024)}, s32[2,128]{1,0:T(2,128)}, /*index=5*/f32[1,768]{1,0:T(1,128)}, bf16[768,2304]{1,0:T(8,128)(2,1)}, s32[128]{0:T(128)}, ...), branch_computations={%region_19.18_spmd, %region_20.0_spmd} | conditional | flops 1896747904 | bytes 45341504 | solution.py:199
  130.3 2.7 constant_dynamic-slice_fusion.3
  133.0 3.4 gather_fusion.2
  143.1 6.3 fusion.72
  149.4 16.7 conditional.2
  152.8 3.3 broadcast_in_dim.218
  156.1 4.1 broadcast_in_dim.221
  160.3 4.8 broadcast_in_dim.220
  170.4 350.8 %collective-permute-start = (bf16[128,768]{1,0:T(8,128)(2,1)}, bf16[128,768]{1,0:T(8,128)(2,1)S(1)}, u32[]{:S(2)}, u32[]{:S(2)}) collective-permute-start(bf16[128,768]{1,0:T(8,128)(2,1)} %get-tuple-element.1699), channel_id=1, source_target_pairs={{0,16},{1,17},{2,18},{3,19},{4,20},{5,21},{6,22},{7,23},{8,24},{9,... | collective-permute-start | bytes 589832 | tf_op jit(solution)/shard_map/while/body/eval_jaxpr/ppermute | solution.py:17
  522.5 4.1 select_add_fusion.15
  526.6 8.9 select_add_fusion.14
  535.5 13.0 select_add_fusion.17
  549.2 11.3 select_add_fusion.18
  563.8 84.3 %conditional.7 = (bf16[128,768]{1,0:T(8,128)(2,1)}, bf16[1024,768]{1,0:T(8,128)(2,1)}, bf16[2048,768]{1,0:T(8,128)(2,1)}, f32[768]{0:T(1024)}, f32[768,2304]{1,0...) conditional(s32[]{:T(128)} %convert_element_type.304, ...), branch_computations={%region_1.17_spmd, %region_18.38_spmd} | conditional | flops 49495343104 | bytes 938855104 | solution.py:258
  577.3 66.5 %conditional.2 = (bf16[2048,768]{1,0:T(8,128)(2,1)}, f32[768]{0:T(1024)}, f32[768,2304]{1,0:T(8,128)}, f32[768,768]{1,0:T(8,128)}, f32[768]{0:T(1024)}, /*index=...) conditional(s32[]{:T(128)} %convert_element_type.172, ...), branch_computations={%region_25.25_spmd, %region_26.37_spmd} | conditional | flops 5622073344 | bytes 209450848 | solution.py:226
  586.1 2.7 convolution_convert_fusion.4
  597.1 4.3 fusion.114
  603.2 4.3 fusion.110
  607.6 2.3 multiply_reduce_fusion.9
  618.8 2.7 fusion.124
  622.1 3.7 scatter_custom_fusion.1
  629.1 4.1 fusion.139
  633.2 5.1 fusion.163
  638.4 5.1 fusion.161
  648.1 328.0 %collective-permute-start = (bf16[128,768]{1,0:T(8,128)(2,1)}, bf16[128,768]{1,0:T(8,128)(2,1)S(1)}, u32[]{:S(2)}, u32[]{:S(2)}) collective-permute-start(bf16[128,768]{1,0:T(8,128)(2,1)} %get-tuple-element.1699), channel_id=1, source_target_pairs={{0,16},{1,17},{2,18},{3,19},{4,20},{5,21},{6,22},{7,23},{8,24},{9,... | collective-permute-start | bytes 589832 | tf_op jit(solution)/shard_map/while/body/eval_jaxpr/ppermute | solution.py:17
  977.5 4.1 select_add_fusion.15
  981.5 8.9 select_add_fusion.14
  990.4 13.0 select_add_fusion.17
  1004.1 11.3 select_add_fusion.18
  1019.0 92.2 %conditional.7 = (bf16[128,768]{1,0:T(8,128)(2,1)}, bf16[1024,768]{1,0:T(8,128)(2,1)}, bf16[2048,768]{1,0:T(8,128)(2,1)}, f32[768]{0:T(1024)}, f32[768,2304]{1,0...) conditional(s32[]{:T(128)} %convert_element_type.304, ...), branch_computations={%region_1.17_spmd, %region_18.38_spmd} | conditional | flops 49495343104 | bytes 938855104 | solution.py:258
  1032.4 74.6 %conditional.2 = (bf16[2048,768]{1,0:T(8,128)(2,1)}, f32[768]{0:T(1024)}, f32[768,2304]{1,0:T(8,128)}, f32[768,768]{1,0:T(8,128)}, f32[768]{0:T(1024)}, /*index=...) conditional(s32[]{:T(128)} %convert_element_type.172, ...), branch_computations={%region_25.25_spmd, %region_26.37_spmd} | conditional | flops 5622073344 | bytes 209450848 | solution.py:226
  1049.0 2.7 convolution_convert_fusion.4
  1060.1 4.3 fusion.114
  1066.2 4.3 fusion.110
  1081.8 2.7 fusion.124
  1085.1 3.7 scatter_custom_fusion.1
  1092.2 4.1 fusion.139
  1096.3 5.1 fusion.163
  1101.4 5.1 fusion.161
  1113.8 4.1 select_add_fusion.15
  1117.9 8.9 select_add_fusion.14
  1126.8 13.0 select_add_fusion.17
  1140.5 11.3 select_add_fusion.18
  1158.9 42.3 %psum.7 = f32[768]{0:T(1024)} all-reduce(f32[768]{0:T(1024)S(1)} %copy-done.91), channel_id=1, replica_groups=mesh['section'=2,'dp'=16] {'section','dp'}, use_global_device_ids=true, to_apply=%region_39.41 | all-reduce | flops 768 | bytes 6144 | tf_op jit(solution)/shard_map/psum | solution.py:286
  1201.3 41.9 %all-reduce.2 = (f32[768]{0:T(1024)S(1)}, f32[768]{0:T(1024)S(1)}) all-reduce(f32[768]{0:T(1024)S(1)} %copy-done.97, f32[768]{0:T(1024)S(1)} %copy-done.94), channel_id=2, replica_groups=mesh['section'=2,'dp'=16] {'dp'}, use_global_device_ids=true, to_apply=%region_40.42.clone | all-reduce | flops 1536 | bytes 12288
  1243.8 43.3 %reduce-scatter.7.cloned.1.call-done = f32[48,768]{1,0:T(8,128)} async-done(((f32[768,768]{1,0:T(8,128)}), f32[48,768]{1,0:T(8,128)}) %reduce-scatter.7.cloned.1.call-update) | async-done | bytes 147472 | tf_op jit(solution)/shard_map/reduce_scatter | solution.py:284
  1287.2 156.4 %reduce-scatter.5.cloned.1.call-done = f32[48,2304]{1,0:T(8,128)} async-done(((f32[768,2304]{1,0:T(8,128)}), f32[48,2304]{1,0:T(8,128)}) %reduce-scatter.5.cloned.1.call-update) | async-done | bytes 442384 | tf_op jit(solution)/shard_map/reduce_scatter | solution.py:284
  1443.5 177.0 %reduce-scatter.9.cloned.1.call-done = f32[48,3072]{1,0:T(8,128)} async-done(((f32[768,3072]{1,0:T(8,128)}), f32[48,3072]{1,0:T(8,128)}) %reduce-scatter.9.cloned.1.call-update) | async-done | bytes 589840 | tf_op jit(solution)/shard_map/reduce_scatter | solution.py:284
  1620.5 176.1 %reduce-scatter.11.cloned.1.call-done = f32[192,768]{1,0:T(8,128)} async-done(((f32[3072,768]{1,0:T(8,128)}), f32[192,768]{1,0:T(8,128)}) %reduce-scatter.11.cloned.1.call-update) | async-done | bytes 589840 | tf_op jit(solution)/shard_map/reduce_scatter | solution.py:284
  (555 shorter events, 138.0 us)
Async XLA Ops:
  7.2 1280.0 %reduce-scatter.7.cloned.1.call-start = ((), (), s32[]{:S(2)}) async-start(), calls=%async_computation.5 | async-start | bytes 2506752 | tf_op jit(solution)/shard_map/reduce_scatter | solution.py:284
  24.4 17.5 copy-start.17
  73.1 33.2 %collective-permute-start = (bf16[128,768]{1,0:T(8,128)(2,1)}, bf16[128,768]{1,0:T(8,128)(2,1)S(1)}, u32[]{:S(2)}, u32[]{:S(2)}) collective-permute-start(bf16[128,768]{1,0:T(8,128)(2,1)} %get-tuple-element.1699), channel_id=1, source_target_pairs={{0,16},{1,17},{2,18},{3,19},{4,20},{5,21},{6,22},{7,23},{8,24},{9,... | collective-permute-start | bytes 589832 | tf_op jit(solution)/shard_map/while/body/eval_jaxpr/ppermute | solution.py:17
  74.4 31.9 %collective-permute-start.1 = (bf16[1024,768]{1,0:T(8,128)(2,1)}, bf16[1024,768]{1,0:T(8,128)(2,1)S(1)}, u32[]{:S(2)}, u32[]{:S(2)}) collective-permute-start(bf16[1024,768]{1,0:T(8,128)(2,1)} %get-tuple-element.1700), channel_id=1, source_target_pairs={{16,0},{17,1},{18,2},{19,3},{20,4},{21,5},{22,6},{23,7},{24,8},{25... | collective-permute-start | bytes 4718600 | tf_op jit(solution)/shard_map/while/body/eval_jaxpr/ppermute | solution.py:17
  85.9 10.3 copy-start.89
  85.9 10.3 copy-start.92
  97.0 8.6 copy-start.90
  97.0 8.6 copy-start.93
  97.0 8.6 copy-start.95
  121.8 17.5 copy-start.17
  170.4 390.8 %collective-permute-start = (bf16[128,768]{1,0:T(8,128)(2,1)}, bf16[128,768]{1,0:T(8,128)(2,1)S(1)}, u32[]{:S(2)}, u32[]{:S(2)}) collective-permute-start(bf16[128,768]{1,0:T(8,128)(2,1)} %get-tuple-element.1699), channel_id=1, source_target_pairs={{0,16},{1,17},{2,18},{3,19},{4,20},{5,21},{6,22},{7,23},{8,24},{9,... | collective-permute-start | bytes 589832 | tf_op jit(solution)/shard_map/while/body/eval_jaxpr/ppermute | solution.py:17
  521.2 40.0 %collective-permute-start.1 = (bf16[1024,768]{1,0:T(8,128)(2,1)}, bf16[1024,768]{1,0:T(8,128)(2,1)S(1)}, u32[]{:S(2)}, u32[]{:S(2)}) collective-permute-start(bf16[1024,768]{1,0:T(8,128)(2,1)} %get-tuple-element.1700), channel_id=1, source_target_pairs={{16,0},{17,1},{18,2},{19,3},{20,4},{21,5},{22,6},{23,7},{24,8},{25... | collective-permute-start | bytes 4718600 | tf_op jit(solution)/shard_map/while/body/eval_jaxpr/ppermute | solution.py:17
  535.5 13.0 copy-start.89
  535.5 13.0 copy-start.92
  549.2 11.3 copy-start.90
  549.2 11.3 copy-start.93
  549.2 11.3 copy-start.95
  578.0 10.8 copy-start.106
  579.4 11.5 copy-start.69
  581.4 10.7 copy-start.60
  582.1 6.7 copy-start.65
  585.8 5.1 copy-start.26
  586.0 7.1 slice-start
  597.1 6.1 copy-start.24
  597.1 6.1 copy-start.30
  601.4 6.1 slice-start.2
  601.8 8.1 copy-start.101
  614.3 4.5 copy-start.18
  616.1 5.4 copy-start.48
  633.2 5.2 copy-start.36
  633.2 5.2 copy-start.80
  648.1 368.0 %collective-permute-start = (bf16[128,768]{1,0:T(8,128)(2,1)}, bf16[128,768]{1,0:T(8,128)(2,1)S(1)}, u32[]{:S(2)}, u32[]{:S(2)}) collective-permute-start(bf16[128,768]{1,0:T(8,128)(2,1)} %get-tuple-element.1699), channel_id=1, source_target_pairs={{0,16},{1,17},{2,18},{3,19},{4,20},{5,21},{6,22},{7,23},{8,24},{9,... | collective-permute-start | bytes 589832 | tf_op jit(solution)/shard_map/while/body/eval_jaxpr/ppermute | solution.py:17
  976.1 40.0 %collective-permute-start.1 = (bf16[1024,768]{1,0:T(8,128)(2,1)}, bf16[1024,768]{1,0:T(8,128)(2,1)S(1)}, u32[]{:S(2)}, u32[]{:S(2)}) collective-permute-start(bf16[1024,768]{1,0:T(8,128)(2,1)} %get-tuple-element.1700), channel_id=1, source_target_pairs={{16,0},{17,1},{18,2},{19,3},{20,4},{21,5},{22,6},{23,7},{24,8},{25... | collective-permute-start | bytes 4718600 | tf_op jit(solution)/shard_map/while/body/eval_jaxpr/ppermute | solution.py:17
  990.4 13.0 copy-start.89
  990.4 13.0 copy-start.92
  1004.1 11.3 copy-start.90
  1004.1 11.3 copy-start.93
  1004.1 11.3 copy-start.95
  1041.0 10.8 copy-start.106
  1042.4 11.5 copy-start.69
  1044.4 10.7 copy-start.60
  1045.1 6.7 copy-start.65
  1048.8 5.1 copy-start.26
  1049.0 7.1 slice-start
  1060.1 6.1 copy-start.24
  1060.1 6.1 copy-start.30
  1064.4 6.1 slice-start.2
  1064.8 8.1 copy-start.101
  1077.3 4.5 copy-start.18
  1079.0 5.4 copy-start.48
  1096.2 5.2 copy-start.36
  1096.2 5.2 copy-start.80
  1111.2 41.3 %collective-permute-start = (bf16[128,768]{1,0:T(8,128)(2,1)}, bf16[128,768]{1,0:T(8,128)(2,1)S(1)}, u32[]{:S(2)}, u32[]{:S(2)}) collective-permute-start(bf16[128,768]{1,0:T(8,128)(2,1)} %get-tuple-element.1699), channel_id=1, source_target_pairs={{0,16},{1,17},{2,18},{3,19},{4,20},{5,21},{6,22},{7,23},{8,24},{9,... | collective-permute-start | bytes 589832 | tf_op jit(solution)/shard_map/while/body/eval_jaxpr/ppermute | solution.py:17
  1112.5 40.0 %collective-permute-start.1 = (bf16[1024,768]{1,0:T(8,128)(2,1)}, bf16[1024,768]{1,0:T(8,128)(2,1)S(1)}, u32[]{:S(2)}, u32[]{:S(2)}) collective-permute-start(bf16[1024,768]{1,0:T(8,128)(2,1)} %get-tuple-element.1700), channel_id=1, source_target_pairs={{16,0},{17,1},{18,2},{19,3},{20,4},{21,5},{22,6},{23,7},{24,8},{25... | collective-permute-start | bytes 4718600 | tf_op jit(solution)/shard_map/while/body/eval_jaxpr/ppermute | solution.py:17
  1126.7 13.0 copy-start.89
  1126.7 13.0 copy-start.92
  1140.5 11.3 copy-start.90
  1140.5 11.3 copy-start.93
  1140.5 11.3 copy-start.95
  1155.5 288.0 %reduce-scatter.5.cloned.1.call-start = ((), (), s32[]{:S(2)}) async-start(), calls=%async_computation.4 | async-start | bytes 7520256 | tf_op jit(solution)/shard_map/reduce_scatter | solution.py:284
  1156.2 464.3 %reduce-scatter.9.cloned.1.call-start = ((), (), s32[]{:S(2)}) async-start(), calls=%async_computation.6 | async-start | bytes 10027008 | tf_op jit(solution)/shard_map/reduce_scatter | solution.py:284
  1157.0 639.7 %reduce-scatter.11.cloned.1.call-start = ((), (), s32[]{:S(2)}) async-start(), calls=%async_computation.7 | async-start | bytes 10027008 | tf_op jit(solution)/shard_map/reduce_scatter | solution.py:284
  1157.0 44.2 %copy-start.94 = (f32[768]{0:T(1024)S(1)}, f32[768]{0:T(1024)}, u32[]{:S(2)}) copy-start(f32[768]{0:T(1024)} %get-tuple-element.1029) | copy-start | bytes 9220
  1157.0 44.2 %copy-start.97 = (f32[768]{0:T(1024)S(1)}, f32[768]{0:T(1024)}, u32[]{:S(2)}) copy-start(f32[768]{0:T(1024)} %get-tuple-element.1026) | copy-start | bytes 9220
  (128 other events, 336.7 us)
Sparse Core Ops, SparseCore 0:
  1155.6 131.5 reduce-scatter.6
  1293.9 149.5 reduce-scatter.4
  1450.7 169.7 reduce-scatter.8
  1626.7 169.9 reduce-scatter.10
where the time goes:
time: 1810 us; the launch traced here: 1800 us
  starting transfers between devices  687 us (38%)
  waiting for transfers between devices  555 us (31%)
  other arithmetic  186 us (10%)
  matrix products  108 us (6%)
  local copies, waits for them, and re-layouts  89.5 us (5%)
  blocking collectives  84.3 us (5%)
  loops' own time  79.4 us (4%)
    ppermute x8, starting transfers between devices, shifted(): lax.ppermute(value, axis, [(source, source + steps) for source in range(i...  687 us
    reduce_scatter x4, waiting for transfers between devices, shards(): lax.psum_scatter(final_state[3], 'dp', scatter_dimension=0, tiled=True)  553 us
    add x20, other arithmetic, tick_step(): running + fresh  144 us
    another operation x4, loops' own time, tick_work(): lax.cond(section_index == 0, routed_tick, dense_tick, tick_index, inbox_f...  63.1 us
    psum x1, blocking collectives, shards(): router_sum = lax.psum(final_state[4], ('section', 'dp'))  42.3 us
    unnamed x1, blocking collectives  41.9 us
  transfers between devices with their start and end apart: 12, of which 4 were waited for; matrix products, arithmetic and copies ran while one was open for 8% of the time, Pallas kernels for 0%

commit v1 on v0

v1 whole, which is shorter than its diff:
```python
import functools

import jax
import jax.numpy as jnp
from jax import lax
from jax.experimental import pallas as pl
from jax.experimental.pallas import tpu as pltpu
from jax.sharding import PartitionSpec as P

HEADS = 12
HEAD_DIM = 64
LANES = 128
PAIRS = HEADS * HEAD_DIM // LANES
EPS = 1e-06
FACTOR = HEAD_DIM ** (-0.5)
PIECES = 16
STAGES = 4
TILE = 256
VMEM_BYTES = 56 * 1024 * 1024
BF16 = jnp.bfloat16
F32 = jnp.float32


def nn(a, b):
    return lax.dot_general(a, b, (((1,), (0,)), ((), ())), preferred_element_type=F32)


def nt(a, b):
    return lax.dot_general(a, b, (((1,), (1,)), ((), ())), preferred_element_type=F32)


def tn(a, b):
    return lax.dot_general(a, b, (((0,), (0,)), ((), ())), preferred_element_type=F32)


def shape(dims, dtype):
    return jax.ShapeDtypeStruct(dims, dtype)


def whole(dims):
    zeros = (0,) * len(dims)
    return pl.BlockSpec(dims, lambda *_: zeros)


ANY = pl.BlockSpec(memory_space=pl.ANY)


def run(body, info, ins, outs, grid, scratch=(), flops=0, moved=0):
    arrays, in_specs = zip(*ins)
    shapes, out_specs = zip(*outs)
    return pl.pallas_call(
        body,
        out_shape=shapes,
        grid_spec=pltpu.PrefetchScalarGridSpec(
            num_scalar_prefetch=1,
            grid=grid,
            in_specs=in_specs,
            out_specs=out_specs,
            scratch_shapes=scratch,
        ),
        compiler_params=pltpu.CompilerParams(
            vmem_limit_bytes=VMEM_BYTES, dimension_semantics=("arbitrary",) * len(grid)
        ),
        cost_estimate=pl.CostEstimate(flops=flops, bytes_accessed=moved, transcendentals=0),
    )(info, *arrays)


def lane_head(rows, which):
    lane = lax.broadcasted_iota(jnp.int32, (rows, LANES), 1)
    return (lane < HEAD_DIM) if which == 0 else (lane >= HEAD_DIM)


def head_only(value, which):
    return jnp.where(lane_head(value.shape[0], which), value, jnp.zeros_like(value))


def mean_square_scale(rows):
    return lax.rsqrt(jnp.mean(rows * rows, axis=-1, keepdims=True) + EPS)


def norm_back(grad, rows, scale, gain):
    hat = rows * scale
    scaled = grad * gain
    back = scale * (scaled - hat * jnp.mean(scaled * hat, axis=-1, keepdims=True))
    return back, jnp.sum(grad * hat, axis=0, keepdims=True)


def gelu_parts(pre):
    root = 0.7978845608028654
    square = pre * pre
    bent = jnp.tanh(root * pre * (1.0 + 0.044715 * square))
    half = 0.5 * (1.0 + bent)
    slope = half + 0.5 * pre * (1.0 - bent * bent) * (root * (1.0 + 0.134145 * square))
    return pre * half, slope


def fetch(info, local, remote, buf, sem):
    @pl.when(info[0] == 1)
    def _():
        pltpu.make_async_copy(local, buf, sem).start()

    @pl.when(info[0] == 0)
    def _():
        pltpu.make_async_copy(remote, buf, sem).start()


def arrived(source, buf, sem):
    pltpu.make_async_copy(source, buf, sem).wait()


def small_attention(packed, seq, pair, allowed):
    cap = allowed.shape[0]
    rows = slice(seq * cap, (seq + 1) * cap)
    width = HEADS * HEAD_DIM
    first = pair * LANES
    queries = packed[rows, first : first + LANES] * BF16(FACTOR)
    keys = packed[rows, width + first : width + first + LANES]
    values = packed[rows, 2 * width + first : 2 * width + first + LANES]
    probs = []
    for head in range(2):
        scores = nt(head_only(queries, head), keys)
        scores = jnp.where(allowed, scores, -1e30)
        top = jnp.max(scores, axis=-1, keepdims=True)
        grown = jnp.exp(scores - top)
        probs.append(grown / jnp.sum(grown, axis=-1, keepdims=True))
    return queries, keys, values, probs


def slot_rule(valid_row, cap):
    query = lax.broadcasted_iota(jnp.int32, (cap, cap), 0)
    key = lax.broadcasted_iota(jnp.int32, (cap, cap), 1)
    return (key <= query) & ((valid_row > 0) | (key == query))


def routed_forward_body(
    info, x, pick_col, valid_row, valid_col, router, gain_attn, gain_mlp, w_qkv, w_out, w_in, w_back,
    chosen_o, normed_o, packed_o, mixed_o, rows_o, mid_o, act_o, slope_o, branch_o, gate_o, delta_o,
    b_qkv, b_out, b_in, b_back, sems,
):
    @pl.when(info[0] == 0)
    def _():
        copies = [
            pltpu.make_async_copy(source, buf, sems.at[n])
            for n, (source, buf) in enumerate(
                ((w_qkv, b_qkv), (w_out, b_out), (w_in, b_in), (w_back, b_back))
            )
        ]
        for copy in copies:
            copy.start()
        seqs, cap = valid_row.shape
        seq_len = x.shape[0] // seqs
        parts = []
        for seq in range(seqs):
            place = lax.broadcasted_iota(jnp.int32, (cap, seq_len), 1)
            hot = (pick_col[seq * cap : (seq + 1) * cap, :] == place).astype(BF16)
            parts.append(nn(hot, x[seq * seq_len : (seq + 1) * seq_len, :]))
        chosen = jnp.concatenate(parts, axis=0)
        chosen_o[...] = chosen.astype(BF16)
        gates = jax.nn.sigmoid(jnp.sum(chosen * router[...], axis=-1, keepdims=True))
        gate_o[...] = jnp.broadcast_to(gates, gate_o.shape)
        normed = (chosen * mean_square_scale(chosen) * gain_attn[...]).astype(BF16)
        normed_o[...] = normed
        copies[0].wait()
        packed_o[...] = nn(normed, b_qkv[...]).astype(BF16)
        for seq in range(seqs):
            allowed = slot_rule(valid_row[seq : seq + 1, :], cap)
            for pair in range(PAIRS):
                _, _, values, probs = small_attention(packed_o, seq, pair, allowed)
                mixed = sum(nn(probs[h].astype(BF16), head_only(values, h)) for h in range(2))
                mixed_o[seq * cap : (seq + 1) * cap, pair * LANES : (pair + 1) * LANES] = (
                    mixed.astype(BF16)
                )
        copies[1].wait()
        attn_out = nn(mixed_o[...], b_out[...])
        rows = chosen + attn_out
        rows_o[...] = rows
        normed_mid = (rows * mean_square_scale(rows) * gain_mlp[...]).astype(BF16)
        mid_o[...] = normed_mid
        copies[2].wait()
        copies[3].wait()
        hidden = b_in.shape[1]
        step = 768
        for first in range(0, hidden, step):
            cols = slice(first, first + step)
            act, slope = gelu_parts(nn(normed_mid, b_in[:, cols]))
            act = act.astype(BF16)
            act_o[:, cols] = act
            slope_o[:, cols] = slope.astype(BF16)
        branch = attn_out + nn(act_o[...], b_back[...])
        branch_o[...] = branch
        delta_o[...] = (gates * valid_col[...].astype(F32) * branch).astype(BF16)


def routed_backward_body(
    info, g_sel, chosen_i, packed, rows_i, slope, branch, gate, valid_row, valid_col, router, gain_attn, gain_mlp,
    w_qkv, w_out, w_in, w_back,
    ffn_o, hidden_o, attn_o, packed_o, chosen_o, small_o,
    b_qkv, b_out, b_in, b_back, sems,
):
    @pl.when(info[0] == 0)
    def _():
        copies = [
            pltpu.make_async_copy(source, buf, sems.at[n])
            for n, (source, buf) in enumerate(
                ((w_qkv, b_qkv), (w_out, b_out), (w_in, b_in), (w_back, b_back))
            )
        ]
        for n in (3, 2, 1, 0):
            copies[n].start()
        seqs, cap = valid_row.shape
        chosen = chosen_i[...].astype(F32)
        grad_sel = g_sel[...].astype(F32)
        gates = gate[:, 0:1]
        mask = valid_col[...].astype(F32)
        logit = jnp.sum(grad_sel * branch[...], axis=-1, keepdims=True) * mask * gates * (1.0 - gates)
        grad = grad_sel * (gates * mask)
        grad_ffn = grad.astype(BF16)
        ffn_o[...] = grad_ffn
        copies[3].wait()
        copies[2].wait()
        step = 768
        for first in range(0, b_in.shape[1], step):
            cols = slice(first, first + step)
            hidden = (nt(grad_ffn, b_back[cols, :]) * slope[:, cols].astype(F32)).astype(BF16)
            hidden_o[:, cols] = hidden
        grad_mid = nt(hidden_o[...], b_in[...])
        rows = rows_i[...]
        grad_rows, gain_mlp_sum = norm_back(grad_mid, rows, mean_square_scale(rows), gain_mlp[...])
        grad_attn = (grad + grad_rows).astype(BF16)
        attn_o[...] = grad_attn
        copies[1].wait()
        grad_mixed = nt(grad_attn, b_out[...]).astype(BF16)
        for seq in range(seqs):
            at = slice(seq * cap, (seq + 1) * cap)
            allowed = slot_rule(valid_row[seq : seq + 1, :], cap)
            for pair in range(PAIRS):
                cols = slice(pair * LANES, (pair + 1) * LANES)
                queries, keys, values, probs = small_attention(packed, seq, pair, allowed)
                grads = grad_mixed[at, cols]
                dq = dk = dv = 0.0
                for head in range(2):
                    grad_head = head_only(grads, head)
                    grad_probs = nt(grad_head, values)
                    prob = probs[head]
                    inner = jnp.sum(prob * grad_probs, axis=-1, keepdims=True)
                    low = (prob * (grad_probs - inner)).astype(BF16)
                    dq = dq + nn(low, head_only(keys, head))
                    dk = dk + tn(low, head_only(queries, head))
                    dv = dv + tn(prob.astype(BF16), grad_head)
                packed_o[0, at, cols] = (dq * FACTOR).astype(BF16)
                packed_o[1, at, cols] = dk.astype(BF16)
                packed_o[2, at, cols] = dv.astype(BF16)
        copies[0].wait()
        width = chosen.shape[1]
        grad_normed = sum(
            nt(packed_o[n], b_qkv[:, n * width : (n + 1) * width]) for n in range(3)
        )
        back, gain_attn_sum = norm_back(grad_normed, chosen, mean_square_scale(chosen), gain_attn[...])
        chosen_o[...] = grad_rows + back + logit * router[...]
        small_o[...] = jnp.zeros(small_o.shape, F32)
        small_o[0:1, :] = jnp.sum(logit * chosen, axis=0, keepdims=True)
        small_o[1:2, :] = gain_mlp_sum
        small_o[2:3, :] = gain_attn_sum


def dense_in_body(info, x, delta, pick_row, gain, w_local, w_far, middle_o, normed_o, packed_o, b_qkv, sem):
    step = pl.program_id(0)

    @pl.when(step == 0)
    def _():
        fetch(info, w_local, w_far, b_qkv, sem)

    rows, width = x.shape
    cap = delta.shape[0]
    place = step * rows + lax.broadcasted_iota(jnp.int32, (rows, cap), 0)
    hot = (pick_row[...] == place).astype(BF16)
    middle = x[...].astype(F32) + nn(hot, delta[...])
    middle_o[...] = middle
    normed = (middle * mean_square_scale(middle) * gain[...]).astype(BF16)
    normed_o[...] = normed

    @pl.when(step == 0)
    def _():
        arrived(w_local, b_qkv, sem)

    for n in range(3):
        packed_o[n] = nn(normed, b_qkv[:, n * width : (n + 1) * width]).astype(BF16)


def attend_forward_body(info, packed, mixed_o, logsum_o):
    seq_len = packed.shape[1]
    queries = packed[0] * BF16(FACTOR)
    keys = packed[1]
    values = [head_only(packed[2], h) for h in range(2)]
    below = lax.broadcasted_iota(jnp.int32, (TILE, TILE), 1) <= lax.broadcasted_iota(
        jnp.int32, (TILE, TILE), 0
    )
    for block in range(seq_len // TILE):
        at = slice(block * TILE, (block + 1) * TILE)
        upto = (block + 1) * TILE
        total = 0.0
        sums = []
        for head in range(2):
            query = head_only(queries[at], head)
            last = jnp.where(below, nt(query, keys[at]), -1e30)
            scores = last
            if block:
                scores = jnp.concatenate([nt(query, keys[: block * TILE]), last], axis=1)
            top = jnp.max(scores, axis=-1, keepdims=True)
            grown = jnp.exp(scores - top)
            row_sum = jnp.sum(grown, axis=-1, keepdims=True)
            total = total + nn(grown.astype(BF16), values[head][:upto]) * (1.0 / row_sum)
            sums.append(top + jnp.log(row_sum))
        mixed_o[at, :] = total.astype(BF16)
        both = jnp.where(lane_head(TILE, 0), sums[0], sums[1])
        turned = jnp.transpose(both)
        logsum_o[0, 0:1, at] = turned[0:1]
        logsum_o[0, 1:2, at] = turned[HEAD_DIM : HEAD_DIM + 1]


def attend_backward_body(info, packed, grad, mixed, logsum, out, grad_q):
    seq_len = packed.shape[1]
    blocks = seq_len // TILE
    queries = packed[0] * BF16(FACTOR)
    queries = [head_only(queries, h) for h in range(2)]
    key_heads = [head_only(packed[1], h) for h in range(2)]
    grads = [head_only(grad[...], h) for h in range(2)]
    product = grad[...].astype(F32) * mixed[...].astype(F32)
    pick_row = lax.broadcasted_iota(jnp.int32, (8, LANES), 0)
    pick_lane = lax.broadcasted_iota(jnp.int32, (8, LANES), 1)
    pick = (pick_row == pick_lane // HEAD_DIM).astype(F32)
    inner = lax.dot_general(
        pick, product, (((1,), (1,)), ((), ())), precision=lax.Precision.HIGHEST, preferred_element_type=F32
    )
    above = lax.broadcasted_iota(jnp.int32, (TILE, TILE), 0) <= lax.broadcasted_iota(
        jnp.int32, (TILE, TILE), 1
    )
    grad_q[...] = jnp.zeros(grad_q.shape, F32)
    for j in range(blocks):
        kat = slice(j * TILE, (j + 1) * TILE)
        keys = packed[1, kat, :]
        values = packed[2, kat, :]
        dk = dv = 0.0
        for i in range(j, blocks):
            qat = slice(i * TILE, (i + 1) * TILE)
            dq = 0.0
            for head in range(2):
                query = queries[head][qat]
                grad_head = grads[head][qat]
                probs = jnp.exp(nt(keys, query) - logsum[0, head : head + 1, qat])
                if i == j:
                    probs = jnp.where(above, probs, 0.0)
                grad_probs = nt(values, grad_head)
                low = (probs * (grad_probs - inner[head : head + 1, qat])).astype(BF16)
                dv = dv + nn(probs.astype(BF16), grad_head)
                dk = dk + nn(low, query)
                dq = dq + tn(low, key_heads[head][kat])
            grad_q[qat, :] += dq
        out[1, kat, :] = dk.astype(BF16)
        out[2, kat, :] = dv.astype(BF16)
    out[0] = (grad_q[...] * FACTOR).astype(BF16)


def feed_body(
    info, mixed, middle, out_grad, gain, wo_l, wo_f, wi_l, wi_f, wb_l, wb_f,
    result_o, act_o, hidden_o, mid_o, carry_o, attn_o, mixed_o, gain_o,
    b_out, b_in, b_back, sems,
):
    step = pl.program_id(0)

    @pl.when(step == 0)
    def _():
        fetch(info, wo_l, wo_f, b_out, sems.at[0])
        fetch(info, wi_l, wi_f, b_in, sems.at[1])
        fetch(info, wb_l, wb_f, b_back, sems.at[2])
        arrived(wo_l, b_out, sems.at[0])

    rows = middle[...] + nn(mixed[...], b_out[...])
    scale = mean_square_scale(rows)
    normed_mid = (rows * scale * gain[...]).astype(BF16)
    mid_o[...] = normed_mid

    @pl.when(step == 0)
    def _():
        arrived(wi_l, b_in, sems.at[1])
        arrived(wb_l, b_back, sems.at[2])

    grad_ffn = out_grad[...]
    width = 768
    for first in range(0, b_in.shape[1], width):
        cols = slice(first, first + width)
        act, slope = gelu_parts(nn(normed_mid, b_in[:, cols]))
        act = act.astype(BF16)
        act_o[:, cols] = act
        hidden = (nt(grad_ffn, b_back[cols, :]) * slope).astype(BF16)
        hidden_o[:, cols] = hidden
    result_o[...] = (rows + nn(act_o[...], b_back[...])).astype(BF16)
    grad_mid = nt(hidden_o[...], b_in[...])
    back, gain_sum = norm_back(grad_mid, rows, scale, gain[...])
    carry = grad_ffn.astype(F32) + back
    carry_o[...] = carry
    grad_attn = carry.astype(BF16)
    attn_o[...] = grad_attn
    mixed_o[...] = nt(grad_attn, b_out[...]).astype(BF16)

    @pl.when(step == 0)
    def _():
        gain_o[...] = jnp.zeros(gain_o.shape, F32)

    gain_o[0:1, :] += gain_sum


def dense_out_body(info, packed, carry, middle, gain, pick_col, w_local, w_far, grad_o, sel_o, gain_o, b_qkv, sem):
    step = pl.program_id(0)

    @pl.when(step == 0)
    def _():
        fetch(info, w_local, w_far, b_qkv, sem)
        gain_o[...] = jnp.zeros(gain_o.shape, F32)
        sel_o[...] = jnp.zeros(sel_o.shape, F32)
        arrived(w_local, b_qkv, sem)

    count, width = middle.shape
    grad_normed = sum(nt(packed[n], b_qkv[:, n * width : (n + 1) * width]) for n in range(3))
    rows = middle[...]
    back, gain_sum = norm_back(grad_normed, rows, mean_square_scale(rows), gain[...])
    gain_o[0:1, :] += gain_sum
    grad = (carry[...] + back).astype(BF16)
    grad_o[...] = grad
    cap = pick_col.shape[0]
    place = step * count + lax.broadcasted_iota(jnp.int32, (cap, count), 1)
    sel_o[...] += nn((pick_col[...] == place).astype(BF16), grad)


def ends_body(info, own, far, grad_chosen, pick_row, out):
    seq = pl.program_id(0)
    step = pl.program_id(1)

    @pl.when(seq == info[0])
    def _():
        out[...] = own[...]

    @pl.when(seq != info[0])
    def _():
        out[...] = far[...]

    @pl.when(info[0] == 0)
    def _():
        rows = out.shape[0]
        cap = grad_chosen.shape[0]
        place = step * rows + lax.broadcasted_iota(jnp.int32, (rows, cap), 0)
        hot = (pick_row[0] == place).astype(F32)
        added = lax.dot_general(
            hot, grad_chosen[...], (((1,), (0,)), ((), ())),
            precision=lax.Precision.HIGHEST, preferred_element_type=F32,
        )
        out[...] = (out[...].astype(F32) + added).astype(BF16)


def position(info, dest):
    relative = info[1] ^ dest
    place = 0
    for stage in range(STAGES):
        place = place * 2 + ((relative >> info[2 + stage]) & 1)
    return place


def chosen_ref(info, refs):
    if len(refs) == 1:
        return refs[0][...]
    return jnp.where(info[0] == 0, refs[0][...], refs[1][...])


def wide_body(count, info, *refs):
    lefts, rights, out, turned = refs[:count], refs[count : 2 * count], refs[-2], refs[-1]

    @pl.when(pl.program_id(0) == 0)
    def _():
        turned[...] = jnp.transpose(chosen_ref(info, lefts))

    right = chosen_ref(info, rights)
    product = nn(turned[...], right.reshape(right.shape[-2:])).astype(BF16)
    piece = out.shape[1]
    for dest in range(PIECES):
        out[position(info, dest)] = product[dest * piece : (dest + 1) * piece, :]


def tall_body(count, info, *refs):
    lefts, rights, out = refs[:count], refs[count : 2 * count], refs[-1]
    step = pl.program_id(0)
    product = tn(chosen_ref(info, lefts), chosen_ref(info, rights)).astype(BF16)
    piece = out.shape[1]
    per_step = product.shape[0] // piece
    for n in range(per_step):
        out[position(info, step * per_step + n)] = product[n * piece : (n + 1) * piece, :]


def wide_product(info, lefts, rights, own, tile):
    depth, rows = lefts[0].shape
    cols = rights[0].shape[-1] * (rights[0].shape[0] if rights[0].ndim == 3 else 1) // 2
    steps = cols // tile

    def half(info_ref):
        return info_ref[0] if own else 1 - info_ref[0]

    if rights[0].ndim == 3:
        fold = rights[0].shape[-1] // tile

        def at(t, info_ref):
            tile_index = t + half(info_ref) * steps
            return (tile_index // fold, 0, tile_index % fold)

        right_spec = pl.BlockSpec((1, depth, tile), at)
    else:
        right_spec = pl.BlockSpec((depth, tile), lambda t, info_ref: (0, t + half(info_ref) * steps))
    return run(
        functools.partial(wide_body, len(lefts)),
        info,
        [(left, whole((depth, rows))) for left in lefts] + [(right, right_spec) for right in rights],
        [
            (
                shape((PIECES, rows // PIECES, cols), BF16),
                pl.BlockSpec((PIECES, rows // PIECES, tile), lambda t, info_ref: (0, 0, t)),
            )
        ],
        (steps,),
        [pltpu.VMEM((rows, depth), BF16)],
        flops=2 * depth * rows * cols,
        moved=2 * (depth * rows + depth * cols + rows * cols),
    )[0]


def tall_product(info, lefts, rights, own):
    depth, rows = lefts[0].shape
    cols = rights[0].shape[1] // 2
    tile = 384
    steps = rows // tile

    def half(info_ref):
        return info_ref[0] if own else 1 - info_ref[0]

    out_dims = (PIECES, rows // PIECES, cols)
    return run(
        functools.partial(tall_body, len(lefts)),
        info,
        [(left, pl.BlockSpec((depth, tile), lambda t, info_ref: (0, t))) for left in lefts]
        + [
            (right, pl.BlockSpec((depth, cols), lambda t, info_ref: (0, half(info_ref))))
            for right in rights
        ],
        [(shape(out_dims, BF16), whole(out_dims))],
        (steps,),
        flops=2 * depth * rows * cols,
        moved=2 * (depth * rows + depth * cols + rows * cols),
    )[0]


def to_section(value, source):
    return lax.ppermute(value, "section", [(source, 1 - source)])


def swap_section(value):
    return lax.ppermute(value, "section", [(0, 1), (1, 0)])


def added_up(parts):
    total = parts[0].astype(F32)
    for part in parts[1:]:
        total = total + part.astype(F32)
    return total


def cross(value, orders, stage, count, low):
    pairs = []
    for section, order in enumerate(orders):
        base = section * count
        flip = low << order[stage]
        pairs += [(base + n, base + (n ^ flip)) for n in range(count)]
    return lax.ppermute(value, ("section", "dp"), pairs)


def scatter_sum(parts, orders):
    count = lax.axis_size("dp")
    low = count // PIECES
    for stage in range(STAGES):
        half = parts[0].shape[0] // 2
        send = added_up([part[half:] for part in parts]).astype(BF16)
        parts = [part[:half] for part in parts] + [cross(send, orders, stage, count, low)]
    own = added_up(parts)[0]
    if low > 1:
        rows, cols = own.shape
        place = lax.axis_index("dp") % low
        pieces = jnp.take(own.reshape(low, rows // low, cols), jnp.arange(low) ^ place, axis=0)
        while pieces.shape[0] > 1:
            half = pieces.shape[0] // 2
            far = lax.ppermute(pieces[half:], "dp", [(n, n ^ half) for n in range(count)])
            pieces = pieces[:half] + far
        own = pieces[0]
    return own


def sum_all(value):
    value = value + swap_section(value)
    count = lax.axis_size("dp")
    flip = 1
    while flip < count:
        value = value + lax.ppermute(value, "dp", [(n, n ^ flip) for n in range(count)])
        flip *= 2
    return value


ORDER_X = (0, 1, 2, 3)
ORDER_Y = (1, 0, 2, 3)
ORDER_Z = (2, 0, 1, 3)
ORDER_W = (2, 1, 0, 3)


def shards(inputs, out_grad, picks, valid, router, gain_attn, w_qkv, w_out, gain_mlp, w_in, w_back):
    w_qkv, w_out, w_in, w_back = w_qkv[0], w_out[0], w_in[0], w_back[0]
    seqs, cap = picks.shape
    seq_len = inputs.shape[0] // seqs
    width = inputs.shape[1]
    hidden = w_in.shape[1]
    rows = seqs * cap
    tiles = seq_len // TILE
    section = lax.axis_index("section")
    low = lax.axis_size("dp") // PIECES
    spot = lax.axis_index("dp") // low
    first = section == 0

    def facts(orders):
        order = jnp.where(first, jnp.array(orders[0]), jnp.array(orders[1]))
        return jnp.concatenate([jnp.stack([section, spot]), order]).astype(jnp.int32)

    info = facts((ORDER_X, ORDER_X))
    far_qkv = to_section(w_qkv, 1)
    far_out = to_section(w_out, 1)
    far_in = to_section(w_in, 1)
    far_back = to_section(w_back, 1)
    pick_col = picks.reshape(rows, 1)
    valid_col = valid.reshape(rows, 1)
    router_row = router.reshape(1, width)

    weight_bufs = [
        pltpu.VMEM(w_qkv.shape, BF16),
        pltpu.VMEM(w_out.shape, BF16),
        pltpu.VMEM(w_in.shape, BF16),
        pltpu.VMEM(w_back.shape, BF16),
        pltpu.SemaphoreType.DMA((4,)),
    ]
    weight_ins = [(w_qkv, ANY), (w_out, ANY), (w_in, ANY), (w_back, ANY)]

    def full(array):
        return (array, whole(array.shape))

    def made(dims, dtype):
        return (shape(dims, dtype), whole(dims))

    routed_flops = 2 * rows * (4 * width * width + 2 * width * hidden)
    weight_bytes = 2 * (4 * width * width + 2 * width * hidden)
    chosen, normed0, packed0, mixed0, rows0, mid0, act0, slope0, branch0, gate0, delta = run(
        routed_forward_body,
        info,
        [full(v) for v in (inputs, pick_col, valid, valid_col, router_row, gain_attn, gain_mlp)] + weight_ins,
        [
            made((rows, width), BF16),
            made((rows, width), BF16),
            made((rows, 3 * width), BF16),
            made((rows, width), BF16),
            made((rows, width), F32),
            made((rows, width), BF16),
            made((rows, hidden), BF16),
            made((rows, hidden), BF16),
            made((rows, width), F32),
            made((rows, LANES), F32),
            made((rows, width), BF16),
        ],
        (1,),
        weight_bufs,
        flops=routed_flops,
        moved=weight_bytes,
    )
    far_delta = to_section(delta[cap:], 0)
    own_delta = jnp.where(first, delta[:cap], far_delta)
    own_picks = jnp.where(first, picks[0], picks[1])
    own_row = own_picks.reshape(1, cap)
    own_col = own_picks.reshape(cap, 1)

    gain_attn1 = jnp.where(first, swap_section(gain_attn), gain_attn)
    gain_mlp1 = jnp.where(first, swap_section(gain_mlp), gain_mlp)

    def row_tile(dims):
        return pl.BlockSpec(dims, lambda i, info_ref: (i, 0))

    def seq_tile():
        return pl.BlockSpec((TILE, width), lambda i, info_ref: (info_ref[0] * tiles + i, 0))

    def tiled(cols, dtype):
        return (shape((seq_len, cols), dtype), row_tile((TILE, cols)))

    three_tile = pl.BlockSpec((3, TILE, width), lambda i, info_ref: (0, i, 0))
    three = shape((3, seq_len, width), BF16)
    qkv_buf = [pltpu.VMEM(w_qkv.shape, BF16), pltpu.SemaphoreType.DMA]

    middle, normed1, packed1 = run(
        dense_in_body,
        info,
        [
            (inputs, seq_tile()),
            full(own_delta),
            full(own_row),
            full(gain_attn1),
            (w_qkv, ANY),
            (far_qkv, ANY),
        ],
        [tiled(width, F32), tiled(width, BF16), (three, three_tile)],
        (tiles,),
        qkv_buf,
        flops=6 * seq_len * width * width,
        moved=seq_len * width * 12 + 6 * width * width,
    )

    pair_spec = pl.BlockSpec((3, seq_len, LANES), lambda h, info_ref: (0, 0, h))
    column_spec = pl.BlockSpec((seq_len, LANES), lambda h, info_ref: (0, h))
    logsum_spec = pl.BlockSpec((1, 8, seq_len), lambda h, info_ref: (h, 0, 0))
    attend_flops = 2 * HEADS * seq_len * seq_len * TILE
    mixed1, logsum1 = run(
        attend_forward_body,
        info,
        [(packed1, pair_spec)],
        [
            (shape((seq_len, width), BF16), column_spec),
            (shape((PAIRS, 8, seq_len), F32), logsum_spec),
        ],
        (PAIRS,),
        flops=attend_flops,
        moved=8 * seq_len * width,
    )

    result, act1, hidden1, mid1, carry, attn1, grad_mixed1, gain_mlp_sum = run(
        feed_body,
        info,
        [
            (mixed1, row_tile((TILE, width))),
            (middle, row_tile((TILE, width))),
            (out_grad, seq_tile()),
            full(gain_mlp1),
            (w_out, ANY),
            (far_out, ANY),
            (w_in, ANY),
            (far_in, ANY),
            (w_back, ANY),
            (far_back, ANY),
        ],
        [
            tiled(width, BF16),
            tiled(hidden, BF16),
            tiled(hidden, BF16),
            tiled(width, BF16),
            tiled(width, F32),
            tiled(width, BF16),
            tiled(width, BF16),
            made((8, width), F32),
        ],
        (tiles,),
        [
            pltpu.VMEM(w_out.shape, BF16),
            pltpu.VMEM(w_in.shape, BF16),
            pltpu.VMEM(w_back.shape, BF16),
            pltpu.SemaphoreType.DMA((3,)),
        ],
        flops=2 * seq_len * width * (2 * width + 4 * hidden),
        moved=seq_len * (20 * width + 4 * hidden) + 2 * width * (width + 2 * hidden),
    )

    out_grad1 = jnp.where(first, out_grad[:seq_len], out_grad[seq_len:])

    def dense_sum(product, orders):
        away = product(facts(orders[::-1]), False)
        return scatter_sum([product(facts(orders), True), swap_section(away)], orders)

    def routed_sum(product, orders):
        return scatter_sum([product(facts(orders), True)], orders)

    sum_in1 = dense_sum(lambda f, own: wide_product(f, [mid1], [hidden1], own, 512), (ORDER_X, ORDER_Y))
    sum_back1 = dense_sum(lambda f, own: tall_product(f, [act1], [out_grad1], own), (ORDER_Z, ORDER_X))

    packed_grad1 = run(
        attend_backward_body,
        info,
        [(packed1, pair_spec), (grad_mixed1, column_spec), (mixed1, column_spec), (logsum1, logsum_spec)],
        [(three, pair_spec)],
        (PAIRS,),
        [pltpu.VMEM((seq_len, LANES), F32)],
        flops=5 * attend_flops // 2,
        moved=16 * seq_len * width,
    )[0]

    sum_out1 = dense_sum(lambda f, own: wide_product(f, [mixed1], [attn1], own, 384), (ORDER_Y, ORDER_W))

    grad_middle, grad_sel, gain_attn_sum = run(
        dense_out_body,
        info,
        [
            (packed_grad1, three_tile),
            (carry, row_tile((TILE, width))),
            (middle, row_tile((TILE, width))),
            full(gain_attn1),
            full(own_col),
            (w_qkv, ANY),
            (far_qkv, ANY),
        ],
        [tiled(width, BF16), made((cap, width), F32), made((8, width), F32)],
        (tiles,),
        qkv_buf,
        flops=6 * seq_len * width * width,
        moved=seq_len * width * 16 + 6 * width * width,
    )
    grad_sel = grad_sel.astype(BF16)
    both_sel = jnp.concatenate([grad_sel, to_section(grad_sel, 1)], axis=0)
    sum_qkv1 = dense_sum(lambda f, own: wide_product(f, [normed1], [packed_grad1], own, 384), (ORDER_Y, ORDER_W))

    ffn0, hidden0, attn0, packed_grad0, grad_chosen, small0 = run(
        routed_backward_body,
        info,
        [
            full(v)
            for v in (
                both_sel, chosen, packed0, rows0, slope0, branch0, gate0, valid, valid_col,
                router_row, gain_attn, gain_mlp,
            )
        ]
        + weight_ins,
        [
            made((rows, width), BF16),
            made((rows, hidden), BF16),
            made((rows, width), BF16),
            made((3, rows, width), BF16),
            made((rows, width), F32),
            made((8, width), F32),
        ],
        (1,),
        weight_bufs,
        flops=routed_flops,
        moved=weight_bytes,
    )

    def both(value):
        return [value, to_section(value, 0)]

    sum_in0 = routed_sum(lambda f, own: wide_product(f, both(mid0), both(hidden0), own, 512), (ORDER_X, ORDER_Y))
    sum_back0 = routed_sum(lambda f, own: tall_product(f, both(act0), both(ffn0), own), (ORDER_Z, ORDER_X))
    sum_out0 = routed_sum(lambda f, own: wide_product(f, both(mixed0), both(attn0), own, 384), (ORDER_Y, ORDER_W))
    sum_qkv0 = routed_sum(
        lambda f, own: wide_product(f, both(normed0), both(packed_grad0), own, 384), (ORDER_Y, ORDER_W)
    )

    far_end = swap_section(jnp.where(first, result, grad_middle))
    own_end = jnp.where(first, grad_middle, result)
    end_spec = pl.BlockSpec((TILE, width), lambda s, i, info_ref: (i, 0))
    ends = run(
        ends_body,
        info,
        [
            (own_end, end_spec),
            (far_end, end_spec),
            (grad_chosen, pl.BlockSpec((cap, width), lambda s, i, info_ref: (s, 0))),
            (picks.reshape(seqs, 1, cap), pl.BlockSpec((1, 1, cap), lambda s, i, info_ref: (s, 0, 0))),
        ],
        [
            (
                shape((seqs * seq_len, width), BF16),
                pl.BlockSpec((TILE, width), lambda s, i, info_ref: (s * tiles + i, 0)),
            )
        ],
        (seqs, tiles),
        flops=4 * seqs * seq_len * cap * width,
        moved=8 * seqs * seq_len * width,
    )[0]

    small = jnp.where(first, small0, 0.0)
    small = jnp.concatenate([small[0:3], gain_mlp_sum[0:1], gain_attn_sum[0:1], small[3:6]], axis=0)
    small = sum_all(small)
    share = width // lax.axis_size("dp")

    def gain_share(routed_row, dense_row):
        row = jnp.where(first, small[routed_row], small[dense_row])
        return lax.dynamic_slice_in_dim(row, lax.axis_index("dp") * share, share)[None]

    def joined(routed, dense):
        far = swap_section(jnp.where(first, dense, routed))
        return jnp.where(
            first,
            jnp.concatenate([routed, far], axis=1),
            jnp.concatenate([far, dense], axis=1),
        )[None]

    return (
        ends[None],
        small[0],
        gain_share(2, 4),
        joined(sum_qkv0, sum_qkv1),
        joined(sum_out0, sum_out1),
        gain_share(1, 3),
        joined(sum_in0, sum_in1),
        joined(sum_back0, sum_back1),
    )


def solution(mesh):
    placed = (
        P("dp", None),
        P("dp", None),
        P("dp", None),
        P("dp", None),
        P(),
        P("section", None),
        P("section", None, None),
        P("section", None, None),
        P("section", None),
        P("section", None, None),
        P("section", None, None),
    )
    return jax.shard_map(
        shards,
        mesh=mesh,
        in_specs=placed,
        out_specs=(
            P("section", "dp", None),
            P(),
            P("section", "dp"),
            P("section", "dp", None),
            P("section", "dp", None),
            P("section", "dp"),
            P("section", "dp", None),
            P("section", "dp", None),
        ),
        check_vma=False,
    )
```

time: 1810 us -> 514 us (0.28)
  starting transfers between devices: 687 us -> 77.6 us
  waiting for transfers between devices: 555 us -> 112 us
  Pallas kernels: 0 us -> 259 us
  other arithmetic: 186 us -> 37.8 us
  matrix products: 108 us -> 0 us
  blocking collectives: 84.3 us -> 0 us
  loops' own time: 79.4 us -> 0 us
  local copies, waits for them, and re-layouts: 89.5 us -> 17.5 us
    ppermute x8 -> x62, starting transfers between devices: 687 us -> 77.6 us  [the longest x32 37.7 us: cross(): return lax.ppermute(value, ('section', 'dp'), pairs)]
    reduce_scatter x4 -> x0, waiting for transfers between devices: 553 us -> none  [shards(): lax.psum_scatter(final_state[3], 'dp', scatter_dimension=0, tiled=True)]
    pallas_call x0 -> x20, Pallas kernels: none -> 259 us  [run(): pl.pallas_call(body, out_shape=shapes, grid_spec=pltpu.PrefetchScalarGrid...]
    add x26 -> x5, other arithmetic: 148 us -> 0.03 us  [the longest x4 0.02 us: sum_all(): value + lax.ppermute(value, 'dp', [(n, n ^ flip) for n in range(count)])]
    ppermute x8 -> x62, waiting for transfers between devices: 0.02 us -> 112 us  [the longest x32 108 us: cross(): return lax.ppermute(value, ('section', 'dp'), pairs)]
    dot_general x52 -> x0, matrix products: 107 us -> none  [the longest x4 21.1 us: block_forward(): ffn_out = jnp.dot(hidden_act, w_back, preferred_element_type=jnp.float32)]
    another operation x13 -> x0, loops' own time: 79.4 us -> none  [the longest x4 63.1 us: tick_work(): lax.cond(section_index == 0, routed_tick, dense_tick, tick_index, inbox_f...]
    psum x1 -> x0, blocking collectives: 42.3 us -> none  [shards(): router_sum = lax.psum(final_state[4], ('section', 'dp'))]
  transfers between devices with their start and end apart: 12 -> 62, of which waited for: 4 -> 21; matrix products, arithmetic and copies ran while one was open for 8% -> 10% of each run, Pallas kernels for 0% -> 51%
where the time goes in v1:
time: 514 us; the launch traced here: 505 us
  Pallas kernels  259 us (50%)
  waiting for transfers between devices  112 us (22%)
  starting transfers between devices  77.6 us (15%)
  other arithmetic  37.8 us (7%)
  local copies, waits for them, and re-layouts  17.5 us (3%)
    pallas_call x20, Pallas kernels, run(): pl.pallas_call(body, out_shape=shapes, grid_spec=pltpu.PrefetchScalarGrid...  259 us
    ppermute x32, waiting for transfers between devices, cross(): return lax.ppermute(value, ('section', 'dp'), pairs)  108 us
    ppermute x32, starting transfers between devices, cross(): return lax.ppermute(value, ('section', 'dp'), pairs)  37.7 us
    ppermute x14, starting transfers between devices, to_section(): return lax.ppermute(value, 'section', [(source, 1 - source)])  27.1 us
    convert_element_type x28, other arithmetic, scatter_sum(): send = added_up([part[half:] for part in parts]).astype(BF16)  18.6 us
  transfers between devices with their start and end apart: 62, of which 21 were waited for; matrix products, arithmetic and copies ran while one was open for 10% of the time, Pallas kernels for 51%

profile of v1, /device:TPU:0, one launch (start us, length us, event | category | flops | bytes accessed | tf_op | source)
XLA Modules:
  0.0 505.2 jit_solution(4632694775880939746)
XLA Ops:
  4.5 7.2 %collective-permute-start.1 = (f32[1,768]{1,0:T(1,128)}, f32[1,768]{1,0:T(1,128)S(1)}, u32[]{:S(2)}, u32[]{:S(2)}) collective-permute-start(f32[1,768]{1,0:T(1,128)} %gain_attn.3), channel_id=1, source_target_pairs={{0,16},{16,0},{1,17},{17,1},{2,18},{18,2},{3,19},{19,3},{4,20},{20... | collective-permute-start | bytes 9224 | tf_op jit(solution)/shard_map/ppermute | solution.py:563
  11.8 1.5 copy.47.valid_col
  14.5 1.5 copy.46.pick_col
  19.3 18.4 %shard_map.404 = (bf16[256,768]{1,0:T(8,128)(2,1)}, bf16[256,768]{1,0:T(8,128)(2,1)}, bf16[256,2304]{1,0:T(8,128)(2,1)}, bf16[256,768]{1,0:T(8,128)(2,1)}, f32[2...) custom-call(s32[6]{0:T(128)} %get-tuple-element.104.info, ...), custom_call_target="tpu_custom_call" | custom-call | flops 3623878656 | bytes 14155776 | tf_op jit(solution)/shard_map/pallas_call | solution.py:51
  40.7 3.1 collective-permute-start
  44.9 3.4 collective-permute-start.50
  48.3 1.6 slice_select_fusion.1.delta
  50.0 1.6 collective-permute-start.26
  51.5 10.6 %shard_map.405 = (f32[1024,768]{1,0:T(8,128)}, bf16[1024,768]{1,0:T(8,128)(2,1)}, bf16[3,1024,768]{2,1,0:T(8,128)(2,1)}) custom-call(s32[6]{0:T(128)} %get-tuple-element.104.info, bf16[2048,768]{1,0:T(8,128)(2,1)} %x.3, bf16[128,768]{1,0:T(8,128)(2,1)} %slice_select_fusion.1.delta, s32[1,128]{1,0:T(1,128)} %broadcast_select_fusion.7.pick_row, ...), custom_call_target="tpu_custom_call" | custom-call | flops 3623878656 | bytes 12976128 | tf_op jit(solution)/shard_map/pallas_call | solution.py:51
  62.1 22.2 %shard_map.406 = (bf16[1024,768]{1,0:T(8,128)(2,1)}, f32[6,8,1024]{2,1,0:T(8,128)}) custom-call(s32[6]{0:T(128)} %get-tuple-element.104.info, bf16[3,1024,768]{2,1,0:T(8,128)(2,1)} %get-tuple-element.42.packed), custom_call_target="tpu_custom_call" | custom-call | flops 6442450944 | bytes 6291456 | tf_op jit(solution)/shard_map/pallas_call | solution.py:51
  85.4 36.6 %shard_map.407 = (bf16[1024,768]{1,0:T(8,128)(2,1)}, bf16[1024,3072]{1,0:T(8,128)(2,1)}, bf16[1024,3072]{1,0:T(8,128)(2,1)}, bf16[1024,768]{1,0:T(8,128)(2,1)}, ...) custom-call(s32[6]{0:T(128)} %get-tuple-element.104.info, ...), custom_call_target="tpu_custom_call" | custom-call | flops 21743271936 | bytes 38928384 | tf_op jit(solution)/shard_map/pallas_call | solution.py:51
  122.0 48.1 %shard_map.408.packed.refs_1_ = bf16[3,1024,768]{2,1,0:T(8,128)(2,1)} custom-call(s32[6]{0:T(128)} %get-tuple-element.104.info, bf16[3,1024,768]{2,1,0:T(8,128)(2,1)} %get-tuple-element.42.packed, bf16[1024,768]{1,0:T(8,128)(2,1)} %get-tuple-element.45.grad, bf16[1024,768]{1,0:T(8,128)(2,1)} %get-tuple-element.43.mixed.refs_0_, ...), custom_call_target="tpu_custom_call" | custom-call | flops 16106127360 | bytes 12582912 | tf_op jit(solution)/shard_map/pallas_call | solution.py:51
  170.1 12.2 %shard_map.409 = (bf16[1024,768]{1,0:T(8,128)(2,1)}, f32[128,768]{1,0:T(8,128)}, f32[8,768]{1,0:T(8,128)}) custom-call(s32[6]{0:T(128)} %get-tuple-element.104.info, bf16[3,1024,768]{2,1,0:T(8,128)(2,1)} %shard_map.408.packed.refs_1_, f32[1024,768]{1,0:T(8,128)} %get-tuple-element.47.carry, f32[1024,768]{1,0:T(8,128)} %get-tuple-element.44.middle, ...), custom_call_target="tpu_custom_call" | custom-call | flops 3623878656 | bytes 16121856 | tf_op jit(solution)/shard_map/pallas_call | solution.py:51
  187.4 4.1 shard_map.417
  192.6 4.1 shard_map.416
  197.4 20.7 %shard_map.410 = (bf16[256,768]{1,0:T(8,128)(2,1)}, bf16[256,3072]{1,0:T(8,128)(2,1)}, bf16[256,768]{1,0:T(8,128)(2,1)}, bf16[3,256,768]{2,1,0:T(8,128)(2,1)}, f32[256,768]{1,0:T(8,128)}, /*index=5*/f32[8,768]{1,0:T(8,128)}) custom-call(s32[6]{0:T(128)} %get-tuple-element.104.info, bf16[256,768]{1,0:T(8,128)(2,1)} %pad_maximum_fusion.g_sel, ...), custom_call_target="tpu_custom_call" | custom-call | flops 3623878656 | bytes 14155776 | tf_op jit(solution)/shard_map/pallas_call | solution.py:51
  219.0 2.4 collective-permute-start.27
  221.5 3.0 collective-permute-start.33
  224.5 1.9 broadcast_select_fusion
  227.8 1.6 collective-permute-start.10
  230.1 3.1 shard_map.415
  235.6 10.2 %shard_map.423 = bf16[16,192,384]{2,1,0:T(8,128)(2,1)} custom-call(s32[6]{0:T(128)} %get-tuple-element.99.info, bf16[1024,3072]{1,0:T(8,128)(2,1)} %get-tuple-element.73.refs_0_, bf16[1024,768]{1,0:T(8,128)(2,1)} %slice_select_fusion.refs_1_), custom_call_target="tpu_custom_call" | custom-call | flops 2415919104 | bytes 9437184 | tf_op jit(solution)/shard_map/pallas_call | solution.py:51
  247.2 2.4 collective-permute-start.15
  250.4 4.4 collective-permute-done.34
  255.5 4.4 collective-permute-done.29
  260.9 3.4 collective-permute-done.35
  265.3 3.3 collective-permute-done.30
  269.5 2.7 collective-permute-start.36
  272.5 2.8 collective-permute-start.31
  275.3 7.2 %shard_map.414 = bf16[16,48,1152]{2,1,0:T(8,128)(2,1)} custom-call(s32[6]{0:T(128)} %get-tuple-element.102.info, bf16[1024,768]{1,0:T(8,128)(2,1)} %get-tuple-element.63.refs_0_, bf16[3,1024,768]{2,1,0:T(8,128)(2,1)} %shard_map.408.packed.refs_1_), custom_call_target="tpu_custom_call" | custom-call | flops 1811939328 | bytes 5701632 | tf_op jit(solution)/shard_map/pallas_call | solution.py:51
  284.8 3.0 collective-permute-done.12
  287.8 10.1 %shard_map.422 = bf16[16,192,384]{2,1,0:T(8,128)(2,1)} custom-call(s32[6]{0:T(128)} %get-tuple-element.77.info, bf16[1024,3072]{1,0:T(8,128)(2,1)} %get-tuple-element.73.refs_0_, bf16[1024,768]{1,0:T(8,128)(2,1)} %slice_select_fusion.refs_1_), custom_call_target="tpu_custom_call" | custom-call | flops 2415919104 | bytes 9437184 | tf_op jit(solution)/shard_map/pallas_call | solution.py:51
  298.6 8.1 %shard_map.421 = bf16[16,192,384]{2,1,0:T(8,128)(2,1)} custom-call(s32[6]{0:T(128)} %get-tuple-element.77.info, bf16[256,3072]{1,0:T(8,128)(2,1)} %get-tuple-element.71.refs_0_, bf16[256,3072]{1,0:T(8,128)(2,1)} %collective-permute-done.50.refs_1_, bf16[256,768]{1,0:T(8,128)(2,1)} %get-tuple-element.72.refs_2_, bf16[256,768]{1,0:T(8,128)(2,1)} %copy-done.21), custom_call_target="tpu_custom_call" | custom-call | flops 603979776 | bytes 4128768 | tf_op jit(solution)/shard_map/pallas_call | solution.py:51
  306.7 2.5 slice.875
  309.2 3.8 collective-permute-start.39
  313.9 7.5 %shard_map.419 = bf16[16,48,1536]{2,1,0:T(8,128)(2,1)} custom-call(s32[6]{0:T(128)} %get-tuple-element.101.info, bf16[1024,768]{1,0:T(8,128)(2,1)} %get-tuple-element.69.refs_0_, bf16[1024,3072]{1,0:T(8,128)(2,1)} %get-tuple-element.70.refs_1_), custom_call_target="tpu_custom_call" | custom-call | flops 2415919104 | bytes 7077888 | tf_op jit(solution)/shard_map/pallas_call | solution.py:51
  321.4 7.1 %shard_map.413 = bf16[16,48,1152]{2,1,0:T(8,128)(2,1)} custom-call(s32[6]{0:T(128)} %get-tuple-element.103.info, bf16[1024,768]{1,0:T(8,128)(2,1)} %get-tuple-element.63.refs_0_, bf16[3,1024,768]{2,1,0:T(8,128)(2,1)} %shard_map.408.packed.refs_1_), custom_call_target="tpu_custom_call" | custom-call | flops 1811939328 | bytes 5701632 | tf_op jit(solution)/shard_map/pallas_call | solution.py:51
  328.5 7.3 %shard_map.420 = bf16[16,48,1536]{2,1,0:T(8,128)(2,1)} custom-call(s32[6]{0:T(128)} %get-tuple-element.100.info, bf16[1024,768]{1,0:T(8,128)(2,1)} %get-tuple-element.69.refs_0_, bf16[1024,3072]{1,0:T(8,128)(2,1)} %get-tuple-element.70.refs_1_), custom_call_target="tpu_custom_call" | custom-call | flops 2415919104 | bytes 7077888 | tf_op jit(solution)/shard_map/pallas_call | solution.py:51
  338.8 5.0 shard_map.412
  343.8 2.2 slice.774
  346.0 10.9 %shard_map.411 = bf16[2048,768]{1,0:T(8,128)(2,1)} custom-call(s32[6]{0:T(128)} %get-tuple-element.104.info, bf16[1024,768]{1,0:T(8,128)(2,1)} %get-tuple-element.89.own, bf16[1024,768]{1,0:T(8,128)(2,1)} %collective-permute-done.7.far, f32[256,768]{1,0:T(8,128)} %get-tuple-element.57.grad_chosen, s32[2,1,128]{2,1,0:T(1,128)} %bitcast.47), custom_call_target="tpu_custom_call" | custom-call | flops 805306368 | bytes 12582912 | tf_op jit(solution)/shard_map/pallas_call | solution.py:51
  356.8 1.5 collective-permute-start.16
  358.4 2.0 add_convert_fusion.4
  361.3 5.4 %shard_map.418 = bf16[16,48,1536]{2,1,0:T(8,128)(2,1)} custom-call(s32[6]{0:T(128)} %get-tuple-element.101.info, bf16[256,768]{1,0:T(8,128)(2,1)} %get-tuple-element.67.refs_0_, bf16[256,768]{1,0:T(8,128)(2,1)} %copy-done.17, bf16[256,3072]{1,0:T(8,128)(2,1)} %get-tuple-element.68.refs_2_, bf16[256,3072]{1,0:T(8,128)(2,1)} %collective-permute-done.39.refs_3_), custom_call_target="tpu_custom_call" | custom-call | flops 603979776 | bytes 3538944 | tf_op jit(solution)/shard_map/pallas_call | solution.py:51
  366.7 1.5 slice.842
  369.5 10.1 %collective-permute-done.16 = bf16[8,48,1152]{2,1,0:T(8,128)(2,1)} collective-permute-done((bf16[8,48,1152]{2,1,0:T(8,128)(2,1)}, bf16[8,48,1152]{2,1,0:T(8,128)(2,1)}, u32[]{:S(2)}, u32[]{:S(2)}) %collective-permute-start.16) | collective-permute-done | bytes 884768 | tf_op jit(solution)/shard_map/ppermute | solution.py:579
  379.7 1.6 collective-permute-start.21
  383.4 1.6 add_convert_fusion
  387.9 1.6 add_convert_fusion.1
  389.4 19.1 %collective-permute-done.54 = bf16[2,192,384]{2,1,0:T(8,128)(2,1)S(1)} collective-permute-done((bf16[2,192,384]{2,1,0:T(8,128)(2,1)S(1)}, bf16[2,192,384]{2,1,0:T(8,128)(2,1)S(1)}, u32[]{:S(2)}, u32[]{:S(2)}) %collective-permute-start.54) | collective-permute-done | bytes 294944 | tf_op jit(solution)/shard_map/ppermute | solution.py:579
  410.6 2.0 collective-permute-start.55
  415.0 16.9 %collective-permute-done.22 = bf16[4,48,1152]{2,1,0:T(8,128)(2,1)S(1)} collective-permute-done((bf16[4,48,1152]{2,1,0:T(8,128)(2,1)S(1)}, bf16[4,48,1152]{2,1,0:T(8,128)(2,1)S(1)}, u32[]{:S(2)}, u32[]{:S(2)}) %collective-permute-start.22) | collective-permute-done | bytes 442400 | tf_op jit(solution)/shard_map/ppermute | solution.py:579
  431.9 1.4 collective-permute-start.18
  433.4 4.4 collective-permute-done.18
  440.2 5.4 %collective-permute-done.23 = bf16[2,48,1152]{2,1,0:T(8,128)(2,1)S(1)} collective-permute-done((bf16[2,48,1152]{2,1,0:T(8,128)(2,1)S(1)}, bf16[2,48,1152]{2,1,0:T(8,128)(2,1)S(1)}, u32[]{:S(2)}, u32[]{:S(2)}) %collective-permute-start.23) | collective-permute-done | bytes 221216 | tf_op jit(solution)/shard_map/ppermute | solution.py:579
  446.0 2.7 collective-permute-start.24
  448.8 2.9 collective-permute-done.19
  452.6 1.5 collective-permute-done.24
  458.9 4.5 collective-permute-done.41
  463.6 8.3 %collective-permute-done.58 = bf16[4,192,384]{2,1,0:T(8,128)(2,1)S(1)} collective-permute-done((bf16[4,192,384]{2,1,0:T(8,128)(2,1)S(1)}, bf16[4,192,384]{2,1,0:T(8,128)(2,1)S(1)}, u32[]{:S(2)}, u32[]{:S(2)}) %collective-permute-start.58) | collective-permute-done | bytes 589856 | tf_op jit(solution)/shard_map/ppermute | solution.py:579
  475.8 3.0 collective-permute-start.43
  481.2 9.1 %collective-permute-done.47 = bf16[2,48,1536]{2,1,0:T(8,128)(2,1)S(1)} collective-permute-done((bf16[2,48,1536]{2,1,0:T(8,128)(2,1)S(1)}, bf16[2,48,1536]{2,1,0:T(8,128)(2,1)S(1)}, u32[]{:S(2)}, u32[]{:S(2)}) %collective-permute-start.47) | collective-permute-done | bytes 294944 | tf_op jit(solution)/shard_map/ppermute | solution.py:579
  491.6 2.4 collective-permute-done.60
  495.4 5.5 %collective-permute-done.48 = bf16[1,48,1536]{2,1,0:T(8,128)(2,1)S(1)} collective-permute-done((bf16[1,48,1536]{2,1,0:T(8,128)(2,1)S(1)}, bf16[1,48,1536]{2,1,0:T(8,128)(2,1)S(1)}, u32[]{:S(2)}, u32[]{:S(2)}) %collective-permute-start.48) | collective-permute-done | bytes 147488 | tf_op jit(solution)/shard_map/ppermute | solution.py:579
  (204 shorter events, 71.8 us)
Async XLA Ops:
  0.6 83.7 %collective-permute-start.5 = (bf16[768,3072]{1,0:T(8,128)(2,1)}, bf16[768,3072]{1,0:T(8,128)(2,1)}, u32[]{:S(2)}, u32[]{:S(2)}) collective-permute-start(bf16[768,3072]{1,0:T(8,128)(2,1)} %bitcast.29), channel_id=1, source_target_pairs={{16,0},{17,1},{18,2},{19,3},{20,4},{21,5},{22,6},{23,7},{24,8},{25... | collective-permute-start | bytes 14155784 | tf_op jit(solution)/shard_map/ppermute | solution.py:559
  1.9 82.5 %collective-permute-start.6 = (bf16[3072,768]{1,0:T(8,128)(2,1)}, bf16[3072,768]{1,0:T(8,128)(2,1)}, u32[]{:S(2)}, u32[]{:S(2)}) collective-permute-start(bf16[3072,768]{1,0:T(8,128)(2,1)} %bitcast.33), channel_id=1, source_target_pairs={{16,0},{17,1},{18,2},{19,3},{20,4},{21,5},{22,6},{23,7},{24,8},{25... | collective-permute-start | bytes 14155784 | tf_op jit(solution)/shard_map/ppermute | solution.py:559
  3.2 46.7 %collective-permute-start.2 = (bf16[768,2304]{1,0:T(8,128)(2,1)}, bf16[768,2304]{1,0:T(8,128)(2,1)}, u32[]{:S(2)}, u32[]{:S(2)}) collective-permute-start(bf16[768,2304]{1,0:T(8,128)(2,1)} %bitcast.24), channel_id=1, source_target_pairs={{16,0},{17,1},{18,2},{19,3},{20,4},{21,5},{22,6},{23,7},{24,8},{25... | collective-permute-start | bytes 10616840 | tf_op jit(solution)/shard_map/ppermute | solution.py:559
  4.5 34.9 %collective-permute-start.1 = (f32[1,768]{1,0:T(1,128)}, f32[1,768]{1,0:T(1,128)S(1)}, u32[]{:S(2)}, u32[]{:S(2)}) collective-permute-start(f32[1,768]{1,0:T(1,128)} %gain_attn.3), channel_id=1, source_target_pairs={{0,16},{16,0},{1,17},{17,1},{2,18},{18,2},{3,19},{19,3},{4,20},{20... | collective-permute-start | bytes 9224 | tf_op jit(solution)/shard_map/ppermute | solution.py:563
  11.8 29.0 %collective-permute-start.3 = (f32[1,768]{1,0:T(1,128)}, f32[1,768]{1,0:T(1,128)S(1)}, u32[]{:S(2)}, u32[]{:S(2)}) collective-permute-start(f32[1,768]{1,0:T(1,128)} %gain_mlp.3), channel_id=1, source_target_pairs={{0,16},{16,0},{1,17},{17,1},{2,18},{18,2},{3,19},{19,3},{4,20},{20... | collective-permute-start | bytes 9224 | tf_op jit(solution)/shard_map/ppermute | solution.py:563
  39.4 44.9 %collective-permute-start.4 = (bf16[768,768]{1,0:T(8,128)(2,1)S(1)}, bf16[768,768]{1,0:T(8,128)(2,1)S(1)}, u32[]{:S(2)}, u32[]{:S(2)}) collective-permute-start(bf16[768,768]{1,0:T(8,128)(2,1)S(1)} %bitcast.40), channel_id=1, source_target_pairs={{16,0},{17,1},{18,2},{19,3},{20,4},{21,5},{22,6},{23,7},{24,8},{25... | collective-permute-start | bytes 3538952 | tf_op jit(solution)/shard_map/ppermute | solution.py:559
  40.7 4.2 collective-permute-start
  44.9 239.8 %collective-permute-start.50 = (bf16[256,3072]{1,0:T(8,128)(2,1)}, bf16[256,3072]{1,0:T(8,128)(2,1)}, u32[]{:S(2)}, u32[]{:S(2)}) collective-permute-start(bf16[256,3072]{1,0:T(8,128)(2,1)} %get-tuple-element.71.refs_0_), channel_id=1, source_target_pairs={{0,16},{1,17},{2,18},{3,19},{4,20},{5,21},{6,22},{7,23},{8,24},{9,... | collective-permute-start | bytes 4718600 | tf_op jit(solution)/shard_map/ppermute | solution.py:559
  50.0 177.8 %collective-permute-start.26 = (bf16[256,768]{1,0:T(8,128)(2,1)}, bf16[256,768]{1,0:T(8,128)(2,1)S(1)}, u32[]{:S(2)}, u32[]{:S(2)}) collective-permute-start(bf16[256,768]{1,0:T(8,128)(2,1)} %get-tuple-element.64.refs_0_), channel_id=1, source_target_pairs={{0,16},{1,17},{2,18},{3,19},{4,20},{5,21},{6,22},{7,23},{8,24},{9,... | collective-permute-start | bytes 1179656 | tf_op jit(solution)/shard_map/ppermute | solution.py:559
  183.3 13.4 %collective-permute-start.8 = (bf16[128,768]{1,0:T(8,128)(2,1)S(1)}, bf16[128,768]{1,0:T(8,128)(2,1)S(1)}, u32[]{:S(2)}, u32[]{:S(2)}) collective-permute-start(bf16[128,768]{1,0:T(8,128)(2,1)S(1)} %convert_element_type.503), channel_id=1, source_target_pairs={{16,0},{17,1},{18,2},{19,3},{20,4},{21,5},{22,6},{23,7},{24,8},{25... | collective-permute-start | bytes 589832 | tf_op jit(solution)/shard_map/ppermute | solution.py:559
  191.4 29.9 %collective-permute-start.32 = (bf16[16,48,384]{2,1,0:T(8,128)(2,1)}, bf16[16,48,384]{2,1,0:T(8,128)(2,1)S(1)}, u32[]{:S(2)}, u32[]{:S(2)}) collective-permute-start(bf16[16,48,384]{2,1,0:T(8,128)(2,1)} %shard_map.417), channel_id=1, source_target_pairs={{0,16},{16,0},{1,17},{17,1},{2,18},{18,2},{3,19},{19,3},{4,20},{20... | collective-permute-start | bytes 1769480 | tf_op jit(solution)/shard_map/ppermute | solution.py:563
  197.4 27.1 %copy-start.13 = (bf16[1024,768]{1,0:T(8,128)(2,1)S(1)}, bf16[1024,768]{1,0:T(8,128)(2,1)}, u32[]{:S(2)}) copy-start(bf16[1024,768]{1,0:T(8,128)(2,1)} %get-tuple-element.48) | copy-start | bytes 4718596
  218.9 7.6 %collective-permute-start.9 = (f32[8,768]{1,0:T(8,128)S(1)}, f32[8,768]{1,0:T(8,128)S(1)}, u32[]{:S(2)}, u32[]{:S(2)}) collective-permute-start(f32[8,768]{1,0:T(8,128)S(1)} %pad_maximum_fusion.1), channel_id=1, source_target_pairs={{0,16},{16,0},{1,17},{17,1},{2,18},{18,2},{3,19},{19,3},{4,20},{20... | collective-permute-start | bytes 73736 | tf_op jit(solution)/shard_map/ppermute | solution.py:563
  219.0 10.4 %collective-permute-start.27 = (bf16[256,768]{1,0:T(8,128)(2,1)}, bf16[256,768]{1,0:T(8,128)(2,1)S(1)}, u32[]{:S(2)}, u32[]{:S(2)}) collective-permute-start(bf16[256,768]{1,0:T(8,128)(2,1)} %get-tuple-element.65.refs_2_), channel_id=1, source_target_pairs={{0,16},{1,17},{2,18},{3,19},{4,20},{5,21},{6,22},{7,23},{8,24},{9,... | collective-permute-start | bytes 1179656 | tf_op jit(solution)/shard_map/ppermute | solution.py:559
  221.5 25.6 %collective-permute-start.33 = (bf16[8,48,384]{2,1,0:T(8,128)(2,1)S(1)}, bf16[8,48,384]{2,1,0:T(8,128)(2,1)S(1)}, u32[]{:S(2)}, u32[]{:S(2)}) collective-permute-start(bf16[8,48,384]{2,1,0:T(8,128)(2,1)S(1)} %add_convert_fusion.13), channel_id=1, source_target_pairs={{0,2},{1,3},{2,0},{3,1},{4,6},{5,7},{6,4},{7,5},{8,10},{9,11},{10,... | collective-permute-start | bytes 884744 | tf_op jit(solution)/shard_map/ppermute | solution.py:579
  226.5 38.7 %collective-permute-start.38 = (bf16[256,768]{1,0:T(8,128)(2,1)S(1)}, bf16[256,768]{1,0:T(8,128)(2,1)S(1)}, u32[]{:S(2)}, u32[]{:S(2)}) collective-permute-start(bf16[256,768]{1,0:T(8,128)(2,1)S(1)} %copy-done.15), channel_id=1, source_target_pairs={{0,16},{1,17},{2,18},{3,19},{4,20},{5,21},{6,22},{7,23},{8,24},{9,... | collective-permute-start | bytes 1179656 | tf_op jit(solution)/shard_map/ppermute | solution.py:559
  227.8 18.0 %collective-permute-start.10 = (f32[8,768]{1,0:T(8,128)S(1)}, f32[8,768]{1,0:T(8,128)S(1)}, u32[]{:S(2)}, u32[]{:S(2)}) collective-permute-start(f32[8,768]{1,0:T(8,128)S(1)} %add.320), channel_id=1, source_target_pairs={{0,1},{1,0},{2,3},{3,2},{4,5},{5,4},{6,7},{7,6},{8,9},{9,8},{10,11... | collective-permute-start | bytes 73736 | tf_op jit(solution)/shard_map/ppermute | solution.py:607
  234.2 15.4 %collective-permute-start.28 = (bf16[8,48,384]{2,1,0:T(8,128)(2,1)S(1)}, bf16[8,48,384]{2,1,0:T(8,128)(2,1)S(1)}, u32[]{:S(2)}, u32[]{:S(2)}) collective-permute-start(bf16[8,48,384]{2,1,0:T(8,128)(2,1)S(1)} %slice.807), channel_id=1, source_target_pairs={{0,2},{1,3},{2,0},{3,1},{4,6},{5,7},{6,4},{7,5},{8,10},{9,11},{10,... | collective-permute-start | bytes 884744 | tf_op jit(solution)/shard_map/ppermute | solution.py:579
  245.8 23.7 %collective-permute-start.14 = (bf16[256,768]{1,0:T(8,128)(2,1)S(1)}, bf16[256,768]{1,0:T(8,128)(2,1)S(1)}, u32[]{:S(2)}, u32[]{:S(2)}) collective-permute-start(bf16[256,768]{1,0:T(8,128)(2,1)S(1)} %copy-done.16), channel_id=1, source_target_pairs={{0,16},{1,17},{2,18},{3,19},{4,20},{5,21},{6,22},{7,23},{8,24},{9,... | collective-permute-start | bytes 1179656 | tf_op jit(solution)/shard_map/ppermute | solution.py:559
  247.2 74.2 %collective-permute-start.15 = (bf16[3,256,768]{2,1,0:T(8,128)(2,1)S(1)}, bf16[3,256,768]{2,1,0:T(8,128)(2,1)}, u32[]{:S(2)}, u32[]{:S(2)}) collective-permute-start(bf16[3,256,768]{2,1,0:T(8,128)(2,1)S(1)} %copy-done.14), channel_id=1, source_target_pairs={{0,16},{1,17},{2,18},{3,19},{4,20},{5,21},{6,22},{7,23},{8,24},{9,... | collective-permute-start | bytes 3538952 | tf_op jit(solution)/shard_map/ppermute | solution.py:559
  249.6 5.2 %collective-permute-start.34 = (bf16[4,48,384]{2,1,0:T(8,128)(2,1)S(1)}, bf16[4,48,384]{2,1,0:T(8,128)(2,1)S(1)}, u32[]{:S(2)}, u32[]{:S(2)}) collective-permute-start(bf16[4,48,384]{2,1,0:T(8,128)(2,1)S(1)} %add_convert_fusion.20), channel_id=1, source_target_pairs={{0,1},{1,0},{2,3},{3,2},{4,5},{5,4},{6,7},{7,6},{8,9},{9,8},{10,11... | collective-permute-start | bytes 442376 | tf_op jit(solution)/shard_map/ppermute | solution.py:579
  254.8 5.1 %collective-permute-start.29 = (bf16[4,48,384]{2,1,0:T(8,128)(2,1)S(1)}, bf16[4,48,384]{2,1,0:T(8,128)(2,1)S(1)}, u32[]{:S(2)}, u32[]{:S(2)}) collective-permute-start(bf16[4,48,384]{2,1,0:T(8,128)(2,1)S(1)} %add_convert_fusion.21), channel_id=1, source_target_pairs={{0,1},{1,0},{2,3},{3,2},{4,5},{5,4},{6,7},{7,6},{8,9},{9,8},{10,11... | collective-permute-start | bytes 442376 | tf_op jit(solution)/shard_map/ppermute | solution.py:579
  260.0 4.4 collective-permute-start.35
  264.3 4.4 collective-permute-start.30
  265.2 71.2 %collective-permute-start.7 = (bf16[1024,768]{1,0:T(8,128)(2,1)}, bf16[1024,768]{1,0:T(8,128)(2,1)}, u32[]{:S(2)}, u32[]{:S(2)}) collective-permute-start(bf16[1024,768]{1,0:T(8,128)(2,1)} %get-tuple-element.88), channel_id=1, source_target_pairs={{0,16},{16,0},{1,17},{17,1},{2,18},{18,2},{3,19},{19,3},{4,20},{20... | collective-permute-start | bytes 4718600 | tf_op jit(solution)/shard_map/ppermute | solution.py:563
  268.7 3.8 collective-permute-start.11
  269.5 13.0 %collective-permute-start.36 = (bf16[1,48,384]{2,1,0:T(8,128)(2,1)S(1)}, bf16[1,48,384]{2,1,0:T(8,128)(2,1)S(1)}, u32[]{:S(2)}, u32[]{:S(2)}) collective-permute-start(bf16[1,48,384]{2,1,0:T(8,128)(2,1)S(1)} %add_convert_fusion.26), channel_id=1, source_target_pairs={{0,8},{1,9},{2,10},{3,11},{4,12},{5,13},{6,14},{7,15},{8,0},{9,1},... | collective-permute-start | bytes 110600 | tf_op jit(solution)/shard_map/ppermute | solution.py:579
  272.5 11.4 %collective-permute-start.31 = (bf16[1,48,384]{2,1,0:T(8,128)(2,1)S(1)}, bf16[1,48,384]{2,1,0:T(8,128)(2,1)S(1)}, u32[]{:S(2)}, u32[]{:S(2)}) collective-permute-start(bf16[1,48,384]{2,1,0:T(8,128)(2,1)S(1)} %add_convert_fusion.27), channel_id=1, source_target_pairs={{0,8},{1,9},{2,10},{3,11},{4,12},{5,13},{6,14},{7,15},{8,0},{9,1},... | collective-permute-start | bytes 110600 | tf_op jit(solution)/shard_map/ppermute | solution.py:579
  282.5 15.3 %collective-permute-start.51 = (bf16[256,768]{1,0:T(8,128)(2,1)S(1)}, bf16[256,768]{1,0:T(8,128)(2,1)S(1)}, u32[]{:S(2)}, u32[]{:S(2)}) collective-permute-start(bf16[256,768]{1,0:T(8,128)(2,1)S(1)} %copy-done.18), channel_id=1, source_target_pairs={{0,16},{1,17},{2,18},{3,19},{4,20},{5,21},{6,22},{7,23},{8,24},{9,... | collective-permute-start | bytes 1179656 | tf_op jit(solution)/shard_map/ppermute | solution.py:559
  283.9 3.9 collective-permute-start.12
  284.7 83.5 %collective-permute-start.20 = (bf16[16,48,1152]{2,1,0:T(8,128)(2,1)}, bf16[16,48,1152]{2,1,0:T(8,128)(2,1)S(1)}, u32[]{:S(2)}, u32[]{:S(2)}) collective-permute-start(bf16[16,48,1152]{2,1,0:T(8,128)(2,1)} %shard_map.414), channel_id=1, source_target_pairs={{0,16},{16,0},{1,17},{17,1},{2,18},{18,2},{3,19},{19,3},{4,20},{20... | collective-permute-start | bytes 5308424 | tf_op jit(solution)/shard_map/ppermute | solution.py:563
  287.7 25.3 %collective-permute-start.37 = (f32[48,384]{1,0:T(8,128)S(1)}, f32[48,384]{1,0:T(8,128)S(1)}, u32[]{:S(2)}, u32[]{:S(2)}) collective-permute-start(f32[48,384]{1,0:T(8,128)S(1)} %get-tuple-element.82), channel_id=1, source_target_pairs={{0,16},{16,0},{1,17},{17,1},{2,18},{18,2},{3,19},{19,3},{4,20},{20... | collective-permute-start | bytes 221192 | tf_op jit(solution)/shard_map/ppermute | solution.py:563
  297.8 11.4 %collective-permute-start.13 = (f32[8,768]{1,0:T(8,128)S(1)}, f32[8,768]{1,0:T(8,128)S(1)}, u32[]{:S(2)}, u32[]{:S(2)}) collective-permute-start(f32[8,768]{1,0:T(8,128)S(1)} %add.323), channel_id=1, source_target_pairs={{0,8},{1,9},{2,10},{3,11},{4,12},{5,13},{6,14},{7,15},{8,0},{9,1},... | collective-permute-start | bytes 73736 | tf_op jit(solution)/shard_map/ppermute | solution.py:607
  309.2 51.1 %collective-permute-start.39 = (bf16[256,3072]{1,0:T(8,128)(2,1)S(1)}, bf16[256,3072]{1,0:T(8,128)(2,1)}, u32[]{:S(2)}, u32[]{:S(2)}) collective-permute-start(bf16[256,3072]{1,0:T(8,128)(2,1)S(1)} %copy-done.11), channel_id=1, source_target_pairs={{0,16},{1,17},{2,18},{3,19},{4,20},{5,21},{6,22},{7,23},{8,24},{9,... | collective-permute-start | bytes 4718600 | tf_op jit(solution)/shard_map/ppermute | solution.py:559
  313.1 43.7 %collective-permute-start.52 = (bf16[8,192,384]{2,1,0:T(8,128)(2,1)}, bf16[8,192,384]{2,1,0:T(8,128)(2,1)}, u32[]{:S(2)}, u32[]{:S(2)}) collective-permute-start(bf16[8,192,384]{2,1,0:T(8,128)(2,1)} %slice.875), channel_id=1, source_target_pairs={{0,4},{1,5},{2,6},{3,7},{4,0},{5,1},{6,2},{7,3},{8,12},{9,13},{10,... | collective-permute-start | bytes 3538952 | tf_op jit(solution)/shard_map/ppermute | solution.py:579
  321.3 61.1 %collective-permute-start.56 = (bf16[16,192,384]{2,1,0:T(8,128)(2,1)S(1)}, bf16[16,192,384]{2,1,0:T(8,128)(2,1)}, u32[]{:S(2)}, u32[]{:S(2)}) collective-permute-start(bf16[16,192,384]{2,1,0:T(8,128)(2,1)S(1)} %copy-done.8), channel_id=1, source_target_pairs={{0,16},{16,0},{1,17},{17,1},{2,18},{18,2},{3,19},{19,3},{4,20},{20... | collective-permute-start | bytes 7077896 | tf_op jit(solution)/shard_map/ppermute | solution.py:563
  336.4 50.2 %collective-permute-start.44 = (bf16[16,48,1536]{2,1,0:T(8,128)(2,1)}, bf16[16,48,1536]{2,1,0:T(8,128)(2,1)}, u32[]{:S(2)}, u32[]{:S(2)}) collective-permute-start(bf16[16,48,1536]{2,1,0:T(8,128)(2,1)} %shard_map.420), channel_id=1, source_target_pairs={{0,16},{16,0},{1,17},{17,1},{2,18},{18,2},{3,19},{19,3},{4,20},{20... | collective-permute-start | bytes 7077896 | tf_op jit(solution)/shard_map/ppermute | solution.py:563
  356.8 22.8 %collective-permute-start.16 = (bf16[8,48,1152]{2,1,0:T(8,128)(2,1)}, bf16[8,48,1152]{2,1,0:T(8,128)(2,1)}, u32[]{:S(2)}, u32[]{:S(2)}) collective-permute-start(bf16[8,48,1152]{2,1,0:T(8,128)(2,1)} %slice.774), channel_id=1, source_target_pairs={{0,2},{1,3},{2,0},{3,1},{4,6},{5,7},{6,4},{7,5},{8,10},{9,11},{10,... | collective-permute-start | bytes 2654216 | tf_op jit(solution)/shard_map/ppermute | solution.py:579
  360.4 24.6 %collective-permute-start.53 = (bf16[4,192,384]{2,1,0:T(8,128)(2,1)}, bf16[4,192,384]{2,1,0:T(8,128)(2,1)}, u32[]{:S(2)}, u32[]{:S(2)}) collective-permute-start(bf16[4,192,384]{2,1,0:T(8,128)(2,1)} %add_convert_fusion.4), channel_id=1, source_target_pairs={{0,1},{1,0},{2,3},{3,2},{4,5},{5,4},{6,7},{7,6},{8,9},{9,8},{10,11... | collective-permute-start | bytes 1769480 | tf_op jit(solution)/shard_map/ppermute | solution.py:579
  368.2 77.7 %collective-permute-start.40 = (bf16[8,48,1536]{2,1,0:T(8,128)(2,1)S(1)}, bf16[8,48,1536]{2,1,0:T(8,128)(2,1)S(1)}, u32[]{:S(2)}, u32[]{:S(2)}) collective-permute-start(bf16[8,48,1536]{2,1,0:T(8,128)(2,1)S(1)} %slice.842), channel_id=1, source_target_pairs={{0,1},{1,0},{2,3},{3,2},{4,5},{5,4},{6,7},{7,6},{8,9},{9,8},{10,11... | collective-permute-start | bytes 3538952 | tf_op jit(solution)/shard_map/ppermute | solution.py:579
  379.7 31.0 %collective-permute-start.21 = (bf16[8,48,1152]{2,1,0:T(8,128)(2,1)S(1)}, bf16[8,48,1152]{2,1,0:T(8,128)(2,1)S(1)}, u32[]{:S(2)}, u32[]{:S(2)}) collective-permute-start(bf16[8,48,1152]{2,1,0:T(8,128)(2,1)S(1)} %add_convert_fusion.2), channel_id=1, source_target_pairs={{0,2},{1,3},{2,0},{3,1},{4,6},{5,7},{6,4},{7,5},{8,10},{9,11},{10,... | collective-permute-start | bytes 2654216 | tf_op jit(solution)/shard_map/ppermute | solution.py:579
  382.4 30.5 %collective-permute-start.17 = (bf16[4,48,1152]{2,1,0:T(8,128)(2,1)S(1)}, bf16[4,48,1152]{2,1,0:T(8,128)(2,1)S(1)}, u32[]{:S(2)}, u32[]{:S(2)}) collective-permute-start(bf16[4,48,1152]{2,1,0:T(8,128)(2,1)S(1)} %add_convert_fusion.8), channel_id=1, source_target_pairs={{0,1},{1,0},{2,3},{3,2},{4,5},{5,4},{6,7},{7,6},{8,9},{9,8},{10,11... | collective-permute-start | bytes 1327112 | tf_op jit(solution)/shard_map/ppermute | solution.py:579
  385.0 70.2 %collective-permute-start.57 = (bf16[8,192,384]{2,1,0:T(8,128)(2,1)S(1)}, bf16[8,192,384]{2,1,0:T(8,128)(2,1)S(1)}, u32[]{:S(2)}, u32[]{:S(2)}) collective-permute-start(bf16[8,192,384]{2,1,0:T(8,128)(2,1)S(1)} %add_convert_fusion), channel_id=1, source_target_pairs={{0,4},{1,5},{2,6},{3,7},{4,0},{5,1},{6,2},{7,3},{8,12},{9,13},{10,... | collective-permute-start | bytes 3538952 | tf_op jit(solution)/shard_map/ppermute | solution.py:579
  386.7 21.9 %collective-permute-start.54 = (bf16[2,192,384]{2,1,0:T(8,128)(2,1)S(1)}, bf16[2,192,384]{2,1,0:T(8,128)(2,1)S(1)}, u32[]{:S(2)}, u32[]{:S(2)}) collective-permute-start(bf16[2,192,384]{2,1,0:T(8,128)(2,1)S(1)} %add_convert_fusion.10), channel_id=1, source_target_pairs={{0,2},{1,3},{2,0},{3,1},{4,6},{5,7},{6,4},{7,5},{8,10},{9,11},{10,... | collective-permute-start | bytes 884744 | tf_op jit(solution)/shard_map/ppermute | solution.py:579
  408.6 49.0 %collective-permute-start.45 = (bf16[8,48,1536]{2,1,0:T(8,128)(2,1)S(1)}, bf16[8,48,1536]{2,1,0:T(8,128)(2,1)S(1)}, u32[]{:S(2)}, u32[]{:S(2)}) collective-permute-start(bf16[8,48,1536]{2,1,0:T(8,128)(2,1)S(1)} %add_convert_fusion.1), channel_id=1, source_target_pairs={{0,1},{1,0},{2,3},{3,2},{4,5},{5,4},{6,7},{7,6},{8,9},{9,8},{10,11... | collective-permute-start | bytes 3538952 | tf_op jit(solution)/shard_map/ppermute | solution.py:579
  410.6 81.0 %collective-permute-start.55 = (bf16[1,192,384]{2,1,0:T(8,128)(2,1)S(1)}, bf16[1,192,384]{2,1,0:T(8,128)(2,1)S(1)}, u32[]{:S(2)}, u32[]{:S(2)}) collective-permute-start(bf16[1,192,384]{2,1,0:T(8,128)(2,1)S(1)} %add_convert_fusion.17), channel_id=1, source_target_pairs={{0,8},{1,9},{2,10},{3,11},{4,12},{5,13},{6,14},{7,15},{8,0},{9,1},... | collective-permute-start | bytes 442376 | tf_op jit(solution)/shard_map/ppermute | solution.py:579
  412.9 35.8 %copy-start.3 = (bf16[16,48,1536]{2,1,0:T(8,128)(2,1)S(1)}, bf16[16,48,1536]{2,1,0:T(8,128)(2,1)}, u32[]{:S(2)}) copy-start(bf16[16,48,1536]{2,1,0:T(8,128)(2,1)} %shard_map.418) | copy-start | bytes 7077892
  412.9 19.0 %collective-permute-start.22 = (bf16[4,48,1152]{2,1,0:T(8,128)(2,1)S(1)}, bf16[4,48,1152]{2,1,0:T(8,128)(2,1)S(1)}, u32[]{:S(2)}, u32[]{:S(2)}) collective-permute-start(bf16[4,48,1152]{2,1,0:T(8,128)(2,1)S(1)} %add_convert_fusion.7), channel_id=1, source_target_pairs={{0,1},{1,0},{2,3},{3,2},{4,5},{5,4},{6,7},{7,6},{8,9},{9,8},{10,11... | collective-permute-start | bytes 1327112 | tf_op jit(solution)/shard_map/ppermute | solution.py:579
  431.9 5.9 %collective-permute-start.18 = (bf16[2,48,1152]{2,1,0:T(8,128)(2,1)S(1)}, bf16[2,48,1152]{2,1,0:T(8,128)(2,1)S(1)}, u32[]{:S(2)}, u32[]{:S(2)}) collective-permute-start(bf16[2,48,1152]{2,1,0:T(8,128)(2,1)S(1)} %add_convert_fusion.15), channel_id=1, source_target_pairs={{0,4},{1,5},{2,6},{3,7},{4,0},{5,1},{6,2},{7,3},{8,12},{9,13},{10,... | collective-permute-start | bytes 663560 | tf_op jit(solution)/shard_map/ppermute | solution.py:579
  437.8 7.7 %collective-permute-start.23 = (bf16[2,48,1152]{2,1,0:T(8,128)(2,1)S(1)}, bf16[2,48,1152]{2,1,0:T(8,128)(2,1)S(1)}, u32[]{:S(2)}, u32[]{:S(2)}) collective-permute-start(bf16[2,48,1152]{2,1,0:T(8,128)(2,1)S(1)} %add_convert_fusion.14), channel_id=1, source_target_pairs={{0,4},{1,5},{2,6},{3,7},{4,0},{5,1},{6,2},{7,3},{8,12},{9,13},{10,... | collective-permute-start | bytes 663560 | tf_op jit(solution)/shard_map/ppermute | solution.py:579
  445.6 6.1 %collective-permute-start.19 = (bf16[1,48,1152]{2,1,0:T(8,128)(2,1)S(1)}, bf16[1,48,1152]{2,1,0:T(8,128)(2,1)S(1)}, u32[]{:S(2)}, u32[]{:S(2)}) collective-permute-start(bf16[1,48,1152]{2,1,0:T(8,128)(2,1)S(1)} %add_convert_fusion.23), channel_id=1, source_target_pairs={{0,8},{1,9},{2,10},{3,11},{4,12},{5,13},{6,14},{7,15},{8,0},{9,1},... | collective-permute-start | bytes 331784 | tf_op jit(solution)/shard_map/ppermute | solution.py:579
  446.0 8.1 %collective-permute-start.24 = (bf16[1,48,1152]{2,1,0:T(8,128)(2,1)S(1)}, bf16[1,48,1152]{2,1,0:T(8,128)(2,1)S(1)}, u32[]{:S(2)}, u32[]{:S(2)}) collective-permute-start(bf16[1,48,1152]{2,1,0:T(8,128)(2,1)S(1)} %add_convert_fusion.22), channel_id=1, source_target_pairs={{0,8},{1,9},{2,10},{3,11},{4,12},{5,13},{6,14},{7,15},{8,0},{9,1},... | collective-permute-start | bytes 331784 | tf_op jit(solution)/shard_map/ppermute | solution.py:579
  451.7 11.7 %collective-permute-start.41 = (bf16[4,48,1536]{2,1,0:T(8,128)(2,1)S(1)}, bf16[4,48,1536]{2,1,0:T(8,128)(2,1)S(1)}, u32[]{:S(2)}, u32[]{:S(2)}) collective-permute-start(bf16[4,48,1536]{2,1,0:T(8,128)(2,1)S(1)} %add_convert_fusion.6), channel_id=1, source_target_pairs={{0,2},{1,3},{2,0},{3,1},{4,6},{5,7},{6,4},{7,5},{8,10},{9,11},{10,... | collective-permute-start | bytes 1769480 | tf_op jit(solution)/shard_map/ppermute | solution.py:579
  455.1 47.0 %collective-permute-start.25 = (f32[48,1152]{1,0:T(8,128)S(1)}, f32[48,1152]{1,0:T(8,128)S(1)}, u32[]{:S(2)}, u32[]{:S(2)}) collective-permute-start(f32[48,1152]{1,0:T(8,128)S(1)} %get-tuple-element.85), channel_id=1, source_target_pairs={{0,16},{16,0},{1,17},{17,1},{2,18},{18,2},{3,19},{19,3},{4,20},{20... | collective-permute-start | bytes 663560 | tf_op jit(solution)/shard_map/ppermute | solution.py:563
  456.5 15.4 %collective-permute-start.58 = (bf16[4,192,384]{2,1,0:T(8,128)(2,1)S(1)}, bf16[4,192,384]{2,1,0:T(8,128)(2,1)S(1)}, u32[]{:S(2)}, u32[]{:S(2)}) collective-permute-start(bf16[4,192,384]{2,1,0:T(8,128)(2,1)S(1)} %add_convert_fusion.3), channel_id=1, source_target_pairs={{0,1},{1,0},{2,3},{3,2},{4,5},{5,4},{6,7},{7,6},{8,9},{9,8},{10,11... | collective-permute-start | bytes 1769480 | tf_op jit(solution)/shard_map/ppermute | solution.py:579
  458.9 15.3 %collective-permute-start.46 = (bf16[4,48,1536]{2,1,0:T(8,128)(2,1)S(1)}, bf16[4,48,1536]{2,1,0:T(8,128)(2,1)S(1)}, u32[]{:S(2)}, u32[]{:S(2)}) collective-permute-start(bf16[4,48,1536]{2,1,0:T(8,128)(2,1)S(1)} %add_convert_fusion.5), channel_id=1, source_target_pairs={{0,2},{1,3},{2,0},{3,1},{4,6},{5,7},{6,4},{7,5},{8,10},{9,11},{10,... | collective-permute-start | bytes 1769480 | tf_op jit(solution)/shard_map/ppermute | solution.py:579
  463.5 12.2 %collective-permute-start.42 = (bf16[2,48,1536]{2,1,0:T(8,128)(2,1)S(1)}, bf16[2,48,1536]{2,1,0:T(8,128)(2,1)S(1)}, u32[]{:S(2)}, u32[]{:S(2)}) collective-permute-start(bf16[2,48,1536]{2,1,0:T(8,128)(2,1)S(1)} %add_convert_fusion.12), channel_id=1, source_target_pairs={{0,4},{1,5},{2,6},{3,7},{4,0},{5,1},{6,2},{7,3},{8,12},{9,13},{10,... | collective-permute-start | bytes 884744 | tf_op jit(solution)/shard_map/ppermute | solution.py:579
  473.0 6.8 %collective-permute-start.59 = (bf16[2,192,384]{2,1,0:T(8,128)(2,1)S(1)}, bf16[2,192,384]{2,1,0:T(8,128)(2,1)S(1)}, u32[]{:S(2)}, u32[]{:S(2)}) collective-permute-start(bf16[2,192,384]{2,1,0:T(8,128)(2,1)S(1)} %add_convert_fusion.9), channel_id=1, source_target_pairs={{0,2},{1,3},{2,0},{3,1},{4,6},{5,7},{6,4},{7,5},{8,10},{9,11},{10,... | collective-permute-start | bytes 884744 | tf_op jit(solution)/shard_map/ppermute | solution.py:579
  475.3 15.0 %collective-permute-start.47 = (bf16[2,48,1536]{2,1,0:T(8,128)(2,1)S(1)}, bf16[2,48,1536]{2,1,0:T(8,128)(2,1)S(1)}, u32[]{:S(2)}, u32[]{:S(2)}) collective-permute-start(bf16[2,48,1536]{2,1,0:T(8,128)(2,1)S(1)} %add_convert_fusion.11), channel_id=1, source_target_pairs={{0,4},{1,5},{2,6},{3,7},{4,0},{5,1},{6,2},{7,3},{8,12},{9,13},{10,... | collective-permute-start | bytes 884744 | tf_op jit(solution)/shard_map/ppermute | solution.py:579
  475.8 19.6 %collective-permute-start.43 = (bf16[1,48,1536]{2,1,0:T(8,128)(2,1)S(1)}, bf16[1,48,1536]{2,1,0:T(8,128)(2,1)S(1)}, u32[]{:S(2)}, u32[]{:S(2)}) collective-permute-start(bf16[1,48,1536]{2,1,0:T(8,128)(2,1)S(1)} %add_convert_fusion.19), channel_id=1, source_target_pairs={{0,8},{1,9},{2,10},{3,11},{4,12},{5,13},{6,14},{7,15},{8,0},{9,1},... | collective-permute-start | bytes 442376 | tf_op jit(solution)/shard_map/ppermute | solution.py:579
  480.8 13.2 %collective-permute-start.60 = (bf16[1,192,384]{2,1,0:T(8,128)(2,1)S(1)}, bf16[1,192,384]{2,1,0:T(8,128)(2,1)S(1)}, u32[]{:S(2)}, u32[]{:S(2)}) collective-permute-start(bf16[1,192,384]{2,1,0:T(8,128)(2,1)S(1)} %add_convert_fusion.16), channel_id=1, source_target_pairs={{0,8},{1,9},{2,10},{3,11},{4,12},{5,13},{6,14},{7,15},{8,0},{9,1},... | collective-permute-start | bytes 442376 | tf_op jit(solution)/shard_map/ppermute | solution.py:579
  491.4 9.5 %collective-permute-start.48 = (bf16[1,48,1536]{2,1,0:T(8,128)(2,1)S(1)}, bf16[1,48,1536]{2,1,0:T(8,128)(2,1)S(1)}, u32[]{:S(2)}, u32[]{:S(2)}) collective-permute-start(bf16[1,48,1536]{2,1,0:T(8,128)(2,1)S(1)} %add_convert_fusion.18), channel_id=1, source_target_pairs={{0,8},{1,9},{2,10},{3,11},{4,12},{5,13},{6,14},{7,15},{8,0},{9,1},... | collective-permute-start | bytes 442376 | tf_op jit(solution)/shard_map/ppermute | solution.py:579
  495.3 7.7 %collective-permute-start.61 = (f32[192,384]{1,0:T(8,128)S(1)}, f32[192,384]{1,0:T(8,128)S(1)}, u32[]{:S(2)}, u32[]{:S(2)}) collective-permute-start(f32[192,384]{1,0:T(8,128)S(1)} %get-tuple-element.74), channel_id=1, source_target_pairs={{0,16},{16,0},{1,17},{17,1},{2,18},{18,2},{3,19},{19,3},{4,20},{20... | collective-permute-start | bytes 884744 | tf_op jit(solution)/shard_map/ppermute | solution.py:563
  502.0 1.8 collective-permute-start.49
  (25 other events, 299.1 us)
